TPU v7x, 512 devices: a whole 4x4x16 slice. The times are simulated.
512 devices in a mesh: inst: 64 (over x_lo, z, core), tp: 8 (over y, x_hi).
Axes of the slice: x: 4 (x_hi: 2, x_lo: 2; x = x_hi * 2 + x_lo), y: 4, z: 16, core: 2. Of those that a mesh axis runs over, the one named last changes fastest.
Arguments:
- queries: bfloat16 [2, 4, 768, 8192], P(None, None, 'inst', 'tp'), may hold values from -125 to 125
- cache_keys: bfloat16 [2, 768, 128, 1024], P(None, 'inst', None, 'tp'), may hold values from -4.5 to 4.5
- cache_values: bfloat16 [2, 768, 128, 1024], P(None, 'inst', None, 'tp'), may hold values from -6 to 6
- new_keys: bfloat16 [2, 4, 768, 1024], P(None, None, 'inst', 'tp'), may hold values from -8 to 8
- new_values: bfloat16 [2, 4, 768, 1024], P(None, None, 'inst', 'tp'), may hold values from -6 to 6
- kv_pool: bfloat16 [5120, 2, 2, 16, 1024], P('inst', None, None, None, 'tp'), may hold values from -6 to 6
- mig_lengths: int32 [64], replicated, may hold values from 256 to 1024, as said below
- mig_source: int32 [64], replicated, may hold values from 0 to 63, as said below
- mig_target: int32 [64], replicated, may hold values from 0 to 63, as said below
- block_lists: int32 [64, 64], replicated, may hold values from 0 to 79, as said below
- owner_map: int32 [64, 64], replicated, may hold values from 0 to 127
- check_key: bfloat16 [2, 2, 1024, 128], P(None, None, 'tp'), may hold values from -0.5 to 0.5
Outputs:
- attention: bfloat16 [2, 4, 768, 8192], P(None, None, 'inst', 'tp')
- arrived: bfloat16 [4096, 2, 2, 16, 1024], P('inst', None, None, None, 'tp')
- checksums: float32 [128, 128], P('inst')
Inputs may be any that keep to these rules, and one draw needn't show every extreme that they name: `mig_lengths`: some request has exactly 1024 tokens and some exactly 256. `mig_source`: each instance drains exactly one request. `mig_target`: each instance receives exactly one request, never its own. `block_lists`: the slots of one row are distinct.
All inputs are finite; a program needn't handle non-finite values.
Results may differ from a plain program's by a relative error of at most 0.015.
Values may be sent and summed in bfloat16 or wider, within the bound.
No kernel may reach another device: no remote copies, remote signals or barrier semaphores. Data moves between devices by JAX's collectives and lax.ppermute only.
A program may use at most 64 MiB of HBM per device.

v0:
```python
import math

import jax
import jax.numpy as jnp
from jax import lax
from jax.sharding import PartitionSpec as P

HD = 128
SLOTS = 2


def decode_attention(queries, cache_keys, cache_values, new_keys, new_values):
    layers, steps, requests, qwidth = queries.shape
    context = cache_keys.shape[2]
    kwidth = cache_keys.shape[3]
    heads_local = kwidth // HD
    grouping = qwidth // kwidth
    query = queries.reshape(layers, steps, requests, heads_local, grouping, HD)
    keyed = cache_keys.reshape(layers, requests, context, heads_local, HD)
    valued = cache_values.reshape(layers, requests, context, heads_local, HD)
    fresh_keys = new_keys.reshape(layers, steps, requests, heads_local, HD)
    fresh_values = new_values.reshape(layers, steps, requests, heads_local, HD)
    factor = 1.0 / math.sqrt(HD)
    old_scores = (
        jnp.einsum("lsrkgd,lrckd->lsrkgc", query, keyed, preferred_element_type=jnp.float32)
        * factor
    )
    new_scores = (
        jnp.einsum("lsrkgd,ltrkd->lsrkgt", query, fresh_keys, preferred_element_type=jnp.float32)
        * factor
    )
    order = jnp.arange(steps)
    visible = (order[None, :] <= order[:, None])[None, :, None, None, None, :]
    new_scores = jnp.where(visible, new_scores, -1e30)
    highest = jnp.maximum(
        jnp.max(old_scores, axis=-1, keepdims=True), jnp.max(new_scores, axis=-1, keepdims=True)
    )
    old_exp = jnp.exp(old_scores - highest)
    new_exp = jnp.where(visible, jnp.exp(new_scores - highest), 0.0)
    denominator = jnp.sum(old_exp, axis=-1, keepdims=True) + jnp.sum(
        new_exp, axis=-1, keepdims=True
    )
    old_weights = (old_exp / denominator).astype(jnp.bfloat16)
    new_weights = (new_exp / denominator).astype(jnp.bfloat16)
    mixed = jnp.einsum(
        "lsrkgc,lrckd->lsrkgd", old_weights, valued, preferred_element_type=jnp.float32
    )
    mixed = mixed + jnp.einsum(
        "lsrkgt,ltrkd->lsrkgd", new_weights, fresh_values, preferred_element_type=jnp.float32
    )
    return mixed.astype(jnp.bfloat16).reshape(layers, steps, requests, qwidth)


def local(
    queries,
    cache_keys,
    cache_values,
    new_keys,
    new_values,
    kv_pool,
    mig_lengths,
    mig_source,
    mig_target,
    block_lists,
    owner_map,
    check_key,
):
    attention = decode_attention(queries, cache_keys, cache_values, new_keys, new_values)
    members = lax.axis_size("inst")
    place = lax.axis_index("inst")
    request_ids = jnp.arange(mig_source.shape[0], dtype=jnp.int32)
    own_request = jnp.sum(jnp.where(mig_source == place, request_ids, 0))
    incoming = jnp.sum(jnp.where(mig_target == place, request_ids, 0))
    length = mig_lengths[own_request]
    slot_row = block_lists[own_request]
    blocks = kv_pool[slot_row]
    depth = slot_row.shape[0]
    span = kv_pool.shape[3]
    position = jnp.arange(depth)[:, None] * span + jnp.arange(span)[None, :]
    blocks = jnp.where(
        (position < length)[:, None, None, :, None], blocks, jnp.zeros((), blocks.dtype)
    )
    sender = mig_source[incoming]
    share = depth // members
    relays = jnp.arange(members, dtype=jnp.int32)
    grouped = blocks.reshape((members, share) + blocks.shape[1:])
    outgoing = grouped[(relays - place) % members]
    source_of = jnp.sum(
        jnp.where(mig_target[None, :] == relays[:, None], mig_source[None, :], 0), axis=1
    )
    gather_back = (sender + relays) % members
    sectioned = lax.all_to_all(outgoing, "inst", split_axis=0, concat_axis=0, tiled=True)
    landed = lax.all_to_all(sectioned[source_of], "inst", split_axis=0, concat_axis=0, tiled=True)
    landed_all = landed[gather_back]
    arrived = landed_all.reshape(blocks.shape)
    layers = arrived.shape[1]
    heads_local = kv_pool.shape[4] // HD
    grid = arrived.reshape(depth, layers, 2, span, heads_local, HD)
    projection = check_key.reshape(layers, 2, heads_local, HD, check_key.shape[-1])
    projected = jnp.einsum(
        "blktgd,lkgde->blktge", grid, projection, preferred_element_type=jnp.float32
    )
    digest = jnp.sum(jnp.tanh(projected), axis=(1, 2, 3, 4)) / 16.0
    owners = owner_map[incoming]
    table_rows = SLOTS * members
    one_hot = (owners[:, None] == jnp.arange(table_rows)[None, :]).astype(jnp.float32)
    partial_table = jnp.dot(
        one_hot.T, digest, precision=lax.Precision.HIGHEST, preferred_element_type=jnp.float32
    )
    summed = lax.psum(partial_table.astype(jnp.bfloat16), "tp").astype(jnp.float32)
    checksums = lax.psum_scatter(summed, "inst", scatter_dimension=0, tiled=True)
    return (attention, arrived, checksums)


def solution(mesh):
    placed = (
        P(None, None, "inst", "tp"),
        P(None, "inst", None, "tp"),
        P(None, "inst", None, "tp"),
        P(None, None, "inst", "tp"),
        P(None, None, "inst", "tp"),
        P("inst", None, None, None, "tp"),
        P(),
        P(),
        P(),
        P(),
        P(),
        P(None, None, "tp", None),
    )
    return jax.shard_map(
        local,
        mesh=mesh,
        in_specs=placed,
        out_specs=(P(None, None, "inst", "tp"), P("inst", None, None, None, "tp"), P("inst", None)),
        check_vma=False,
    )
```

profile of v0, /device:TPU:2, one launch (start us, length us, event | category | flops | bytes accessed | tf_op | source)
XLA Modules:
  0.0 391.9 jit_solution(1516857713529756190)
XLA Ops:
  0.6 0.0 copy-start
  0.7 1.5 fusion.24
  4.1 0.7 fusion.28
  4.8 1.2 dynamic_slice.12
  6.1 0.0 copy-done
  6.1 0.7 gather_fusion
  6.8 0.7 add_compare_fusion
  7.6 0.2 fusion.5
  7.8 1.7 gather_fusion.1
  9.4 0.0 copy-start.4
  9.4 17.3 %all-to-all-start = ((bf16[64,1,2,2,16,128]{5,4,3,2,1,0:T(8,128)(2,1)}), bf16[64,1,2,2,16,128]{5,4,3,2,1,0:T(8,128)(2,1)S(1)}, u32[]{:S(2)}, u32[]{:S(2)}) async-start(bf16[64,1,2,2,16,128]{5,4,3,2,1,0:T(8,128)(2,1)} %bitcast.24), calls=%async_computation | async-start | bytes 2097152 | tf_op jit(solution)/shard_map/all_to_all | solution.py:92
  26.8 0.0 copy-done.4
  26.8 0.0 copy-done.5
  26.8 0.1 select_reduce_fusion
  26.9 51.9 %all-to-all-done = bf16[64,1,2,2,16,128]{5,4,3,2,1,0:T(8,128)(2,1)S(1)} async-done(((bf16[64,1,2,2,16,128]{5,4,3,2,1,0:T(8,128)(2,1)}), bf16[64,1,2,2,16,128]{5,4,3,2,1,0:T(8,128)(2,1)S(1)}, u32[]{:S(2)}, u32[]{:S(2)}) %all-to-all-start) | async-done | bytes 1048608 | tf_op jit(solution)/shard_map/all_to_all | solution.py:92
  78.8 1.7 gather_fusion.2
  80.5 8.1 %all-to-all-start.1 = ((bf16[64,1,2,2,16,128]{5,4,3,2,1,0:T(8,128)(2,1)}), bf16[64,1,2,2,16,128]{5,4,3,2,1,0:T(8,128)(2,1)S(1)}, u32[]{:S(2)}, u32[]{:S(2)}) async-start(bf16[64,1,2,2,16,128]{5,4,3,2,1,0:T(8,128)(2,1)} %bitcast.29), calls=%async_computation.1 | async-start | bytes 2097152 | tf_op jit(solution)/shard_map/all_to_all | solution.py:93
  90.0 0.0 copy-done.3
  90.0 0.1 reshape.276
  90.1 0.0 copy-start.8
  90.1 0.0 copy-done.2
  90.1 0.0 copy-start.6
  90.1 0.6 fusion.34
  90.7 0.1 copy-done.8
  90.8 1.0 fusion.35
  91.8 0.2 fusion.14
  92.0 0.4 fusion.10
  92.4 0.0 copy-done.6
  92.4 0.0 copy-start.9
  92.4 0.4 fusion.7
  92.8 0.3 copy-done.9
  93.2 0.3 fusion.2
  93.5 0.0 copy-start.7
  93.5 0.7 reshape.279
  95.0 0.6 dynamic_slice.14
  95.5 1.3 dynamic-slice
  97.6 0.7 fusion.31
  98.2 0.7 dynamic-slice_bitcast_fusion
  99.0 41.7 %all-to-all-done.1 = bf16[64,1,2,2,16,128]{5,4,3,2,1,0:T(8,128)(2,1)S(1)} async-done(((bf16[64,1,2,2,16,128]{5,4,3,2,1,0:T(8,128)(2,1)}), bf16[64,1,2,2,16,128]{5,4,3,2,1,0:T(8,128)(2,1)S(1)}, u32[]{:S(2)}, u32[]{:S(2)}) %all-to-all-start.1) | async-done | bytes 1048608 | tf_op jit(solution)/shard_map/all_to_all | solution.py:93
  140.6 0.8 gather_fusion.3
  141.4 0.0 copy-done.7
  141.4 0.0 copy-start.1
  141.4 0.5 tanh_reduce_fusion
  141.9 0.5 copy-done.1
  142.4 0.3 convolution_convert_fusion
  142.7 41.3 %psum.7 = bf16[128,128]{1,0:T(8,128)(2,1)S(1)} all-reduce(bf16[128,128]{1,0:T(8,128)(2,1)S(1)} %convolution_convert_fusion), channel_id=1, replica_groups=mesh['inst'=64,'tp'=8] {'tp'}, use_global_device_ids=true, to_apply=%region_8.9 | all-reduce | flops 16384 | bytes 65536 | tf_op jit(solution)/shard_map/psum | solution.py:110
  184.0 207.4 %all-reduce.2 = f32[128,128]{1,0:T(8,128)S(1)} all-reduce(bf16[128,128]{1,0:T(8,128)(2,1)S(1)} %psum.7), channel_id=2, replica_groups=mesh['inst'=64,'tp'=8] {'inst'}, use_global_device_ids=true, to_apply=%region_9.10.clone | all-reduce | flops 16384 | bytes 98304
  391.4 0.6 constant_dynamic-slice_fusion
  (13 shorter events, 0.1 us)
Async XLA Ops:
  0.6 5.4 %copy-start = (bf16[80,2,2,16,128]{4,3,2,1,0:T(8,128)(2,1)S(1)}, bf16[80,2,2,16,128]{4,3,2,1,0:T(8,128)(2,1)}, u32[]{:S(2)}) copy-start(bf16[80,2,2,16,128]{4,3,2,1,0:T(8,128)(2,1)} %param.17) | copy-start | bytes 3932164
  9.4 17.4 %copy-start.4 = (s32[64]{0:T(128)S(1)}, s32[64]{0:T(128)}, u32[]{:S(2)}) copy-start(s32[64]{0:T(128)} %param.20) | copy-start | bytes 772
  9.4 17.4 %copy-start.5 = (s32[64]{0:T(128)S(1)}, s32[64]{0:T(128)}, u32[]{:S(2)}) copy-start(s32[64]{0:T(128)} %param.19) | copy-start | bytes 772
  9.4 69.4 %all-to-all-start = ((bf16[64,1,2,2,16,128]{5,4,3,2,1,0:T(8,128)(2,1)}), bf16[64,1,2,2,16,128]{5,4,3,2,1,0:T(8,128)(2,1)S(1)}, u32[]{:S(2)}, u32[]{:S(2)}) async-start(bf16[64,1,2,2,16,128]{5,4,3,2,1,0:T(8,128)(2,1)} %bitcast.24), calls=%async_computation | async-start | bytes 2097152 | tf_op jit(solution)/shard_map/all_to_all | solution.py:92
  80.5 9.5 %copy-start.3 = (bf16[2,4,12,1024]{3,1,2,0:T(4,128)(2,1)S(1)}, bf16[2,4,12,1024]{3,1,2,0:T(4,128)(2,1)}, u32[]{:S(2)}) copy-start(bf16[2,4,12,1024]{3,1,2,0:T(4,128)(2,1)} %param.12) | copy-start | bytes 589828
  80.5 9.6 %copy-start.2 = (bf16[2,12,128,128]{3,2,1,0:T(8,128)(2,1)S(1)}, bf16[2,12,128,128]{3,2,1,0:T(8,128)(2,1)}, u32[]{:S(2)}) copy-start(bf16[2,12,128,128]{3,2,1,0:T(8,128)(2,1)} %param.13) | copy-start | bytes 2359300
  80.5 60.1 %all-to-all-start.1 = ((bf16[64,1,2,2,16,128]{5,4,3,2,1,0:T(8,128)(2,1)}), bf16[64,1,2,2,16,128]{5,4,3,2,1,0:T(8,128)(2,1)S(1)}, u32[]{:S(2)}, u32[]{:S(2)}) async-start(bf16[64,1,2,2,16,128]{5,4,3,2,1,0:T(8,128)(2,1)} %bitcast.29), calls=%async_computation.1 | async-start | bytes 2097152 | tf_op jit(solution)/shard_map/all_to_all | solution.py:93
  90.1 0.7 copy-start.8
  90.1 2.3 copy-start.6
  92.4 0.7 copy-start.9
  93.5 47.9 %copy-start.7 = (bf16[2,2,128,128]{3,2,1,0:T(8,128)(2,1)S(1)}, bf16[2,2,128,128]{3,2,1,0:T(8,128)(2,1)}, u32[]{:S(2)}) copy-start(bf16[2,2,128,128]{3,2,1,0:T(8,128)(2,1)} %param.23) | copy-start | bytes 393220
  141.4 1.0 copy-start.1
where the time goes:
time: 393 us; the launch traced here: 392 us
  blocking collectives  249 us (63%)
  waiting for transfers between devices  93.6 us (24%)
  starting transfers between devices  25.4 us (6%)
  local copies, waits for them, and re-layouts  11 us (3%)
  between operations  5.6 us (1%)
  other arithmetic  4.56 us (1%)
    unnamed x1, blocking collectives  207 us
    all_to_all x1, waiting for transfers between devices, local(): lax.all_to_all(outgoing, 'inst', split_axis=0, concat_axis=0, tiled=True)  51.9 us
    all_to_all x1, waiting for transfers between devices, local(): lax.all_to_all(sectioned[source_of], 'inst', split_axis=0, concat_axis=0,...  41.7 us
    psum x1, blocking collectives, local(): lax.psum(partial_table.astype(jnp.bfloat16), 'tp').astype(jnp.float32)  41.3 us
    all_to_all x1, starting transfers between devices, local(): lax.all_to_all(outgoing, 'inst', split_axis=0, concat_axis=0, tiled=True)  17.3 us
    all_to_all x1, starting transfers between devices, local(): lax.all_to_all(sectioned[source_of], 'inst', split_axis=0, concat_axis=0,...  8.07 us
  transfers between devices with their start and end apart: 2, of which 2 were waited for; matrix products, arithmetic and copies ran while one was open for 2% of the time, Pallas kernels for 0%

commit v1 on v0

--- a/solution.py
+++ b/solution.py
@@ -67,48 +67,41 @@
 ):
     attention = decode_attention(queries, cache_keys, cache_values, new_keys, new_values)
     members = lax.axis_size("inst")
+    heads = lax.axis_size("tp")
     place = lax.axis_index("inst")
     request_ids = jnp.arange(mig_source.shape[0], dtype=jnp.int32)
     own_request = jnp.sum(jnp.where(mig_source == place, request_ids, 0))
-    incoming = jnp.sum(jnp.where(mig_target == place, request_ids, 0))
     length = mig_lengths[own_request]
     slot_row = block_lists[own_request]
     blocks = kv_pool[slot_row]
-    depth = slot_row.shape[0]
-    span = kv_pool.shape[3]
+    depth, layers, pair, span, width = blocks.shape
     position = jnp.arange(depth)[:, None] * span + jnp.arange(span)[None, :]
     blocks = jnp.where(
         (position < length)[:, None, None, :, None], blocks, jnp.zeros((), blocks.dtype)
     )
-    sender = mig_source[incoming]
-    share = depth // members
-    relays = jnp.arange(members, dtype=jnp.int32)
-    grouped = blocks.reshape((members, share) + blocks.shape[1:])
-    outgoing = grouped[(relays - place) % members]
+    sectioned = lax.all_to_all(blocks, "inst", split_axis=0, concat_axis=0, tiled=True)
+
+    projected = jnp.einsum("blktd,lkde->blkte", blocks, check_key, preferred_element_type=jnp.float32)
+    digest = jnp.sum(jnp.tanh(projected), axis=(1, 2, 3)) / 16.0
+    owners = owner_map[own_request]
+    table_rows = SLOTS * members
+    one_hot = (owners[None, :] == jnp.arange(table_rows)[:, None]).astype(jnp.float32)
+    table = jnp.dot(one_hot, digest, precision=lax.Precision.HIGHEST, preferred_element_type=jnp.float32)
+    reach = 1
+    while reach < heads:
+        table = table + lax.ppermute(table, "tp", [(i, i ^ reach) for i in range(heads)])
+        reach *= 2
+    terms = table.astype(jnp.bfloat16).reshape(members, 1, SLOTS, table.shape[-1])
+
     source_of = jnp.sum(
-        jnp.where(mig_target[None, :] == relays[:, None], mig_source[None, :], 0), axis=1
+        jnp.where(mig_target[None, :] == request_ids[:, None], mig_source[None, :], 0), axis=1
     )
-    gather_back = (sender + relays) % members
-    sectioned = lax.all_to_all(outgoing, "inst", split_axis=0, concat_axis=0, tiled=True)
-    landed = lax.all_to_all(sectioned[source_of], "inst", split_axis=0, concat_axis=0, tiled=True)
-    landed_all = landed[gather_back]
-    arrived = landed_all.reshape(blocks.shape)
-    layers = arrived.shape[1]
-    heads_local = kv_pool.shape[4] // HD
-    grid = arrived.reshape(depth, layers, 2, span, heads_local, HD)
-    projection = check_key.reshape(layers, 2, heads_local, HD, check_key.shape[-1])
-    projected = jnp.einsum(
-        "blktgd,lkgde->blktge", grid, projection, preferred_element_type=jnp.float32
+    onward = sectioned[source_of].reshape(members, -1, SLOTS, width)
+    landed = lax.all_to_all(
+        jnp.concatenate([onward, terms], axis=1), "inst", split_axis=0, concat_axis=0, tiled=True
     )
-    digest = jnp.sum(jnp.tanh(projected), axis=(1, 2, 3, 4)) / 16.0
-    owners = owner_map[incoming]
-    table_rows = SLOTS * members
-    one_hot = (owners[:, None] == jnp.arange(table_rows)[None, :]).astype(jnp.float32)
-    partial_table = jnp.dot(
-        one_hot.T, digest, precision=lax.Precision.HIGHEST, preferred_element_type=jnp.float32
-    )
-    summed = lax.psum(partial_table.astype(jnp.bfloat16), "tp").astype(jnp.float32)
-    checksums = lax.psum_scatter(summed, "inst", scatter_dimension=0, tiled=True)
+    arrived = landed[:, :-1].reshape(blocks.shape)
+    checksums = jnp.sum(landed[:, -1].astype(jnp.float32), axis=0)
     return (attention, arrived, checksums)
 
 

time: 393 us -> 148 us (0.38)
  the two profiles are of different devices: /device:TPU:2 before, /device:TPU:57 now
where the time goes in v1:
time: 148 us
  waiting for transfers between devices  92.5 us (62%)
  starting transfers between devices  32.5 us (22%)
  other arithmetic  7.81 us (5%)
  local copies, waits for them, and re-layouts  7.68 us (5%)
  matrix products  4.23 us (3%)
  between operations  2.82 us (2%)
    all_to_all x1, waiting for transfers between devices, local(): lax.all_to_all(jnp.concatenate([onward, terms], axis=1), 'inst', split_ax...  50.6 us
    all_to_all x1, waiting for transfers between devices, local(): lax.all_to_all(blocks, 'inst', split_axis=0, concat_axis=0, tiled=True)  32.7 us
    all_to_all x1, starting transfers between devices, local(): lax.all_to_all(blocks, 'inst', split_axis=0, concat_axis=0, tiled=True)  17.1 us
    ppermute x3, starting transfers between devices, local(): lax.ppermute(table, 'tp', [(i, i ^ reach) for i in range(heads)])  9.59 us
    ppermute x3, waiting for transfers between devices, local(): lax.ppermute(table, 'tp', [(i, i ^ reach) for i in range(heads)])  9.24 us
    all_to_all x1, starting transfers between devices, local(): lax.all_to_all(jnp.concatenate([onward, terms], axis=1), 'inst', split_ax...  5.79 us
  transfers between devices with their start and end apart: 5, of which 5 were waited for; matrix products, arithmetic and copies ran while one was open for 5% of the time, Pallas kernels for 0%

profile of v1, /device:TPU:57, one launch (start us, length us, event | category | flops | bytes accessed | tf_op | source)
XLA Modules:
  0.0 147.6 jit_solution(3926146886902657063)
XLA Ops:
  0.6 0.0 copy-start
  0.7 1.4 fusion.24
  4.0 0.7 fusion.25
  4.7 1.2 dynamic_slice.9
  5.9 0.0 copy-done
  6.0 0.7 gather_fusion
  6.7 0.7 add_compare_fusion
  7.4 1.2 broadcast_select_fusion
  8.6 0.0 copy-start.3
  8.6 17.1 %all-to-all-start = ((bf16[64,2,2,16,128]{4,3,2,1,0:T(8,128)(2,1)}), bf16[64,2,2,16,128]{4,3,2,1,0:T(8,128)(2,1)S(1)}, u32[]{:S(2)}, u32[]{:S(2)}) async-start(bf16[64,2,2,16,128]{4,3,2,1,0:T(8,128)(2,1)} %broadcast_select_fusion), calls=%async_computation | async-start | bytes 2097152 | tf_op jit(solution)/shard_map/all_to_all | solution.py:82
  25.8 0.7 dynamic-slice_bitcast_fusion
  26.5 0.0 copy-done.3
  26.5 0.0 copy-start.6
  26.5 0.0 copy-start.7
  26.5 1.7 %tanh_reduce_fusion = f32[64,128]{1,0:T(8,128)S(1)} fusion(bf16[64,2,2,16,128]{4,3,2,1,0:T(8,128)(2,1)} %broadcast_select_fusion, bf16[2,2,128,128]{3,2,1,0:T(8,128)(2,1)S(1)} %copy-done.3), kind=kOutput, calls=%fused_computation.2 | convolution fusion | flops 134733824 | bytes 1212416 | tf_op jit(solution)/shard_map/blktd,lkde->blkte/dot_general | solution.py:84
  28.2 0.2 fusion.18
  28.4 4.4 %collective-permute-start = (f32[128,128]{1,0:T(8,128)S(1)}, f32[128,128]{1,0:T(8,128)S(1)}, u32[]{:S(2)}, u32[]{:S(2)}) collective-permute-start(f32[128,128]{1,0:T(8,128)S(1)} %fusion.18), channel_id=1, source_target_pairs={{0,1},{1,0},{2,3},{3,2},{4,5},{5,4},{6,7},{7,6},{8,9},{9,8},{10,11... | collective-permute-start | bytes 196616 | tf_op jit(solution)/shard_map/ppermute | solution.py:92
  32.7 0.0 copy-done.6
  32.7 0.0 copy-done.7
  32.7 0.1 select_reduce_fusion
  32.9 2.4 %collective-permute-done = f32[128,128]{1,0:T(8,128)S(1)} collective-permute-done((f32[128,128]{1,0:T(8,128)S(1)}, f32[128,128]{1,0:T(8,128)S(1)}, u32[]{:S(2)}, u32[]{:S(2)}) %collective-permute-start) | collective-permute-done | bytes 65568 | tf_op jit(solution)/shard_map/ppermute | solution.py:92
  35.3 2.4 %collective-permute-start.1 = (f32[128,128]{1,0:T(8,128)S(1)}, f32[128,128]{1,0:T(8,128)S(1)}, u32[]{:S(2)}, u32[]{:S(2)}) collective-permute-start(f32[128,128]{1,0:T(8,128)S(1)} %add.81), channel_id=1, source_target_pairs={{0,2},{1,3},{2,0},{3,1},{4,6},{5,7},{6,4},{7,5},{8,10},{9,11},{10,... | collective-permute-start | bytes 196616 | tf_op jit(solution)/shard_map/ppermute | solution.py:92
  37.7 2.9 %collective-permute-done.1 = f32[128,128]{1,0:T(8,128)S(1)} collective-permute-done((f32[128,128]{1,0:T(8,128)S(1)}, f32[128,128]{1,0:T(8,128)S(1)}, u32[]{:S(2)}, u32[]{:S(2)}) %collective-permute-start.1) | collective-permute-done | bytes 65568 | tf_op jit(solution)/shard_map/ppermute | solution.py:92
  40.6 2.9 %collective-permute-start.2 = (f32[128,128]{1,0:T(8,128)S(1)}, f32[128,128]{1,0:T(8,128)S(1)}, u32[]{:S(2)}, u32[]{:S(2)}) collective-permute-start(f32[128,128]{1,0:T(8,128)S(1)} %add.82), channel_id=1, source_target_pairs={{0,4},{1,5},{2,6},{3,7},{4,0},{5,1},{6,2},{7,3},{8,12},{9,13},{10,... | collective-permute-start | bytes 196616 | tf_op jit(solution)/shard_map/ppermute | solution.py:92
  43.5 3.9 %collective-permute-done.2 = f32[128,128]{1,0:T(8,128)S(1)} collective-permute-done((f32[128,128]{1,0:T(8,128)S(1)}, f32[128,128]{1,0:T(8,128)S(1)}, u32[]{:S(2)}, u32[]{:S(2)}) %collective-permute-start.2) | collective-permute-done | bytes 65568 | tf_op jit(solution)/shard_map/ppermute | solution.py:92
  47.4 32.7 %all-to-all-done = bf16[64,2,2,16,128]{4,3,2,1,0:T(8,128)(2,1)S(1)} async-done(((bf16[64,2,2,16,128]{4,3,2,1,0:T(8,128)(2,1)}), bf16[64,2,2,16,128]{4,3,2,1,0:T(8,128)(2,1)S(1)}, u32[]{:S(2)}, u32[]{:S(2)}) %all-to-all-start) | async-done | bytes 1048608 | tf_op jit(solution)/shard_map/all_to_all | solution.py:82
  80.1 0.7 gather_fusion.1
  80.8 2.4 %pad_maximum_fusion = bf16[64,33,2,128]{3,2,1,0:T(2,128)(2,1)} fusion(bf16[64,1,2,128]{3,2,1,0:T(2,128)(2,1)S(1)} %bitcast.77, bf16[64,32,2,128]{3,2,1,0:T(2,128)(2,1)S(1)} %bitcast.75), kind=kLoop, calls=%fused_computation.11 | loop fusion | flops 540672 | bytes 2162688 | tf_op jit(solution)/shard_map/concatenate | solution.py:101
  83.2 0.0 copy-start.1
  83.2 5.8 %all-to-all-start.1 = ((bf16[64,33,2,128]{3,2,1,0:T(2,128)(2,1)}), bf16[64,33,2,128]{3,2,1,0:T(2,128)(2,1)S(1)}, u32[]{:S(2)}, u32[]{:S(2)}) async-start(bf16[64,33,2,128]{3,2,1,0:T(2,128)(2,1)} %pad_maximum_fusion), calls=%async_computation.1 | async-start | bytes 2162688 | tf_op jit(solution)/shard_map/all_to_all | solution.py:100
  89.0 0.0 copy-start.4
  89.1 1.0 reshape.169
  90.1 0.0 copy-done.1
  90.1 0.6 fusion.29
  90.7 0.0 copy-done.4
  90.7 0.0 copy-start.2
  90.7 1.0 fusion.30
  91.7 0.2 fusion.13
  92.0 0.4 fusion.9
  92.4 0.0 copy-done.2
  92.4 0.0 copy-start.5
  92.4 0.4 fusion.6
  92.8 0.3 copy-done.5
  93.1 0.3 fusion.2
  93.5 0.7 reshape.172
  94.2 50.6 %all-to-all-done.1 = bf16[64,33,2,128]{3,2,1,0:T(2,128)(2,1)S(1)} async-done(((bf16[64,33,2,128]{3,2,1,0:T(2,128)(2,1)}), bf16[64,33,2,128]{3,2,1,0:T(2,128)(2,1)S(1)}, u32[]{:S(2)}, u32[]{:S(2)}) %all-to-all-start.1) | async-done | bytes 1081376 | tf_op jit(solution)/shard_map/all_to_all | solution.py:100
  144.8 2.1 %slice.12 = bf16[64,32,2,128]{3,2,1,0:T(2,128)(2,1)} slice(bf16[64,33,2,128]{3,2,1,0:T(2,128)(2,1)S(1)} %all-to-all-done.1), slice={[0:64], [0:32], [0:2], [0:128]} | slice | bytes 2097152 | tf_op jit(solution)/shard_map/slice | solution.py:103
  146.9 0.6 convert_reduce_fusion
  (10 shorter events, 0.1 us)
Async XLA Ops:
  0.6 5.3 %copy-start = (bf16[80,2,2,16,128]{4,3,2,1,0:T(8,128)(2,1)S(1)}, bf16[80,2,2,16,128]{4,3,2,1,0:T(8,128)(2,1)}, u32[]{:S(2)}) copy-start(bf16[80,2,2,16,128]{4,3,2,1,0:T(8,128)(2,1)} %param.17) | copy-start | bytes 3932164
  8.6 17.8 %copy-start.3 = (bf16[2,2,128,128]{3,2,1,0:T(8,128)(2,1)S(1)}, bf16[2,2,128,128]{3,2,1,0:T(8,128)(2,1)}, u32[]{:S(2)}) copy-start(bf16[2,2,128,128]{3,2,1,0:T(8,128)(2,1)} %param.23) | copy-start | bytes 393220
  8.6 71.5 %all-to-all-start = ((bf16[64,2,2,16,128]{4,3,2,1,0:T(8,128)(2,1)}), bf16[64,2,2,16,128]{4,3,2,1,0:T(8,128)(2,1)S(1)}, u32[]{:S(2)}, u32[]{:S(2)}) async-start(bf16[64,2,2,16,128]{4,3,2,1,0:T(8,128)(2,1)} %broadcast_select_fusion), calls=%async_computation | async-start | bytes 2097152 | tf_op jit(solution)/shard_map/all_to_all | solution.py:82
  26.5 6.3 %copy-start.6 = (s32[64]{0:T(128)S(1)}, s32[64]{0:T(128)}, u32[]{:S(2)}) copy-start(s32[64]{0:T(128)} %param.19) | copy-start | bytes 772
  26.5 6.3 %copy-start.7 = (s32[64]{0:T(128)S(1)}, s32[64]{0:T(128)}, u32[]{:S(2)}) copy-start(s32[64]{0:T(128)} %param.20) | copy-start | bytes 772
  28.4 6.9 %collective-permute-start = (f32[128,128]{1,0:T(8,128)S(1)}, f32[128,128]{1,0:T(8,128)S(1)}, u32[]{:S(2)}, u32[]{:S(2)}) collective-permute-start(f32[128,128]{1,0:T(8,128)S(1)} %fusion.18), channel_id=1, source_target_pairs={{0,1},{1,0},{2,3},{3,2},{4,5},{5,4},{6,7},{7,6},{8,9},{9,8},{10,11... | collective-permute-start | bytes 196616 | tf_op jit(solution)/shard_map/ppermute | solution.py:92
  35.3 5.3 %collective-permute-start.1 = (f32[128,128]{1,0:T(8,128)S(1)}, f32[128,128]{1,0:T(8,128)S(1)}, u32[]{:S(2)}, u32[]{:S(2)}) collective-permute-start(f32[128,128]{1,0:T(8,128)S(1)} %add.81), channel_id=1, source_target_pairs={{0,2},{1,3},{2,0},{3,1},{4,6},{5,7},{6,4},{7,5},{8,10},{9,11},{10,... | collective-permute-start | bytes 196616 | tf_op jit(solution)/shard_map/ppermute | solution.py:92
  40.6 6.8 %collective-permute-start.2 = (f32[128,128]{1,0:T(8,128)S(1)}, f32[128,128]{1,0:T(8,128)S(1)}, u32[]{:S(2)}, u32[]{:S(2)}) collective-permute-start(f32[128,128]{1,0:T(8,128)S(1)} %add.82), channel_id=1, source_target_pairs={{0,4},{1,5},{2,6},{3,7},{4,0},{5,1},{6,2},{7,3},{8,12},{9,13},{10,... | collective-permute-start | bytes 196616 | tf_op jit(solution)/shard_map/ppermute | solution.py:92
  83.2 6.8 %copy-start.1 = (bf16[2,12,128,128]{3,2,1,0:T(8,128)(2,1)S(1)}, bf16[2,12,128,128]{3,2,1,0:T(8,128)(2,1)}, u32[]{:S(2)}) copy-start(bf16[2,12,128,128]{3,2,1,0:T(8,128)(2,1)} %param.13) | copy-start | bytes 2359300
  83.2 61.5 %all-to-all-start.1 = ((bf16[64,33,2,128]{3,2,1,0:T(2,128)(2,1)}), bf16[64,33,2,128]{3,2,1,0:T(2,128)(2,1)S(1)}, u32[]{:S(2)}, u32[]{:S(2)}) async-start(bf16[64,33,2,128]{3,2,1,0:T(2,128)(2,1)} %pad_maximum_fusion), calls=%async_computation.1 | async-start | bytes 2162688 | tf_op jit(solution)/shard_map/all_to_all | solution.py:100
  89.0 1.7 %copy-start.4 = (bf16[2,4,12,128]{3,1,2,0:T(4,128)(2,1)S(1)}, bf16[2,4,12,128]{3,1,2,0:T(4,128)(2,1)}, u32[]{:S(2)}) copy-start(bf16[2,4,12,128]{3,1,2,0:T(4,128)(2,1)} %param.15) | copy-start | bytes 73732
  90.7 1.6 %copy-start.2 = (bf16[2,12,128,128]{3,2,1,0:T(8,128)(2,1)S(1)}, bf16[2,12,128,128]{3,2,1,0:T(8,128)(2,1)}, u32[]{:S(2)}) copy-start(bf16[2,12,128,128]{3,2,1,0:T(8,128)(2,1)} %param.14) | copy-start | bytes 2359300
  92.4 0.7 copy-start.5

commit v2 on v1

--- a/solution.py
+++ b/solution.py
@@ -74,7 +74,7 @@
     length = mig_lengths[own_request]
     slot_row = block_lists[own_request]
     blocks = kv_pool[slot_row]
-    depth, layers, pair, span, width = blocks.shape
+    depth, span = blocks.shape[0], blocks.shape[3]
     position = jnp.arange(depth)[:, None] * span + jnp.arange(span)[None, :]
     blocks = jnp.where(
         (position < length)[:, None, None, :, None], blocks, jnp.zeros((), blocks.dtype)
@@ -87,21 +87,29 @@
     table_rows = SLOTS * members
     one_hot = (owners[None, :] == jnp.arange(table_rows)[:, None]).astype(jnp.float32)
     table = jnp.dot(one_hot, digest, precision=lax.Precision.HIGHEST, preferred_element_type=jnp.float32)
+    part = table
+    reach = members // 2
+    while reach:
+        half = part.shape[0] // 2
+        upper = (place // reach) % 2 == 1
+        low, high = part[:half], part[half:]
+        away = jnp.where(upper, low, high)
+        part = jnp.where(upper, high, low) + lax.ppermute(
+            away, "inst", [(i, i ^ reach) for i in range(members)]
+        )
+        reach //= 2
     reach = 1
     while reach < heads:
-        table = table + lax.ppermute(table, "tp", [(i, i ^ reach) for i in range(heads)])
+        part = part + lax.ppermute(part, "tp", [(i, i ^ reach) for i in range(heads)])
         reach *= 2
-    terms = table.astype(jnp.bfloat16).reshape(members, 1, SLOTS, table.shape[-1])
+    checksums = part
 
     source_of = jnp.sum(
         jnp.where(mig_target[None, :] == request_ids[:, None], mig_source[None, :], 0), axis=1
     )
-    onward = sectioned[source_of].reshape(members, -1, SLOTS, width)
-    landed = lax.all_to_all(
-        jnp.concatenate([onward, terms], axis=1), "inst", split_axis=0, concat_axis=0, tiled=True
+    arrived = lax.all_to_all(
+        sectioned[source_of], "inst", split_axis=0, concat_axis=0, tiled=True
     )
-    arrived = landed[:, :-1].reshape(blocks.shape)
-    checksums = jnp.sum(landed[:, -1].astype(jnp.float32), axis=0)
     return (attention, arrived, checksums)
 
 

time: 148 us -> 193 us (1.30)
  the two profiles are of different devices: /device:TPU:57 before, /device:TPU:30 now
where the time goes in v2:
time: 193 us; the launch traced here: 192 us
  waiting for transfers between devices  108 us (56%)
  starting transfers between devices  57 us (30%)
  other arithmetic  8.94 us (5%)
  matrix products  8.9 us (5%)
  local copies, waits for them, and re-layouts  6.16 us (3%)
  between operations  2.94 us (2%)
    ppermute x6, waiting for transfers between devices, local(): lax.ppermute(away, 'inst', [(i, i ^ reach) for i in range(members)])  52.5 us
    all_to_all x1, waiting for transfers between devices, local(): lax.all_to_all(blocks, 'inst', split_axis=0, concat_axis=0, tiled=True)  49.5 us
    ppermute x6, starting transfers between devices, local(): lax.ppermute(away, 'inst', [(i, i ^ reach) for i in range(members)])  22.4 us
    all_to_all x1, starting transfers between devices, local(): lax.all_to_all(blocks, 'inst', split_axis=0, concat_axis=0, tiled=True)  17.3 us
    ppermute x3, starting transfers between devices, local(): lax.ppermute(part, 'tp', [(i, i ^ reach) for i in range(heads)])  9.21 us
    all_to_all x1, starting transfers between devices, local(): lax.all_to_all(sectioned[source_of], 'inst', split_axis=0, concat_axis=0,...  8.07 us
    ppermute x3, waiting for transfers between devices, local(): lax.ppermute(part, 'tp', [(i, i ^ reach) for i in range(heads)])  6.47 us
  transfers between devices with their start and end apart: 11, of which 10 were waited for; matrix products, arithmetic and copies ran while one was open for 8% of the time, Pallas kernels for 0%

profile of v2, /device:TPU:30, one launch (start us, length us, event | category | flops | bytes accessed | tf_op | source)
XLA Modules:
  0.0 192.4 jit_solution(10529756902983024664)
XLA Ops:
  0.6 0.0 copy-start
  0.7 1.4 fusion.24
  4.0 0.7 fusion.25
  4.7 1.2 dynamic_slice.9
  6.0 0.7 gather_fusion
  6.7 0.7 add_compare_fusion
  7.4 1.2 broadcast_select_fusion
  8.6 17.3 %all-to-all-start = ((bf16[64,2,2,16,128]{4,3,2,1,0:T(8,128)(2,1)}), bf16[64,2,2,16,128]{4,3,2,1,0:T(8,128)(2,1)S(1)}, u32[]{:S(2)}, u32[]{:S(2)}) async-start(bf16[64,2,2,16,128]{4,3,2,1,0:T(8,128)(2,1)} %broadcast_select_fusion), calls=%async_computation | async-start | bytes 2097152 | tf_op jit(solution)/shard_map/all_to_all | solution.py:82
  26.0 0.7 dynamic-slice_bitcast_fusion
  26.7 0.1 select_reduce_fusion
  26.8 1.7 tanh_reduce_fusion
  28.5 49.5 %all-to-all-done = bf16[64,2,2,16,128]{4,3,2,1,0:T(8,128)(2,1)S(1)} async-done(((bf16[64,2,2,16,128]{4,3,2,1,0:T(8,128)(2,1)}), bf16[64,2,2,16,128]{4,3,2,1,0:T(8,128)(2,1)S(1)}, u32[]{:S(2)}, u32[]{:S(2)}) %all-to-all-start) | async-done | bytes 1048608 | tf_op jit(solution)/shard_map/all_to_all | solution.py:82
  78.0 1.6 gather_fusion.1
  79.7 8.1 %all-to-all-start.1 = ((bf16[64,2,2,16,128]{4,3,2,1,0:T(8,128)(2,1)}), bf16[64,2,2,16,128]{4,3,2,1,0:T(8,128)(2,1)S(1)}, u32[]{:S(2)}, u32[]{:S(2)}) async-start(bf16[64,2,2,16,128]{4,3,2,1,0:T(8,128)(2,1)} %gather_fusion.1), calls=%async_computation.1 | async-start | bytes 2097152 | tf_op jit(solution)/shard_map/all_to_all | solution.py:110
  87.8 0.2 fusion.18
  88.0 2.4 %collective-permute-start = (f32[64,128]{1,0:T(8,128)S(1)}, f32[64,128]{1,0:T(8,128)S(1)}, u32[]{:S(2)}, u32[]{:S(2)}) collective-permute-start(f32[64,128]{1,0:T(8,128)S(1)} %slice_select_fusion), channel_id=1, source_target_pairs={{0,256},{8,264},{16,272},{24,280},{32,288},{40,296},{48,304},{56,3... | collective-permute-start | bytes 98312 | tf_op jit(solution)/shard_map/ppermute | solution.py:97
  90.4 3.9 %collective-permute-done = f32[64,128]{1,0:T(8,128)S(1)} collective-permute-done((f32[64,128]{1,0:T(8,128)S(1)}, f32[64,128]{1,0:T(8,128)S(1)}, u32[]{:S(2)}, u32[]{:S(2)}) %collective-permute-start) | collective-permute-done | bytes 32800 | tf_op jit(solution)/shard_map/ppermute | solution.py:97
  94.3 11.9 %collective-permute-start.1 = (f32[32,128]{1,0:T(8,128)S(1)}, f32[32,128]{1,0:T(8,128)S(1)}, u32[]{:S(2)}, u32[]{:S(2)}) collective-permute-start(f32[32,128]{1,0:T(8,128)S(1)} %slice_select_fusion.1), channel_id=1, source_target_pairs={{0,128},{8,136},{16,144},{24,152},{32,160},{40,168},{48,176},{56,1... | collective-permute-start | bytes 49160 | tf_op jit(solution)/shard_map/ppermute | solution.py:97
  106.2 39.0 %collective-permute-done.1 = f32[32,128]{1,0:T(8,128)S(1)} collective-permute-done((f32[32,128]{1,0:T(8,128)S(1)}, f32[32,128]{1,0:T(8,128)S(1)}, u32[]{:S(2)}, u32[]{:S(2)}) %collective-permute-start.1) | collective-permute-done | bytes 16416 | tf_op jit(solution)/shard_map/ppermute | solution.py:97
  145.2 0.6 slice_select_fusion.2
  145.8 1.9 collective-permute-start.2
  147.7 0.5 iota_compare_fusion.3
  148.2 0.1 reshape.159
  148.3 0.0 copy-start.2
  148.3 7.2 %collective-permute-done.2 = f32[16,128]{1,0:T(8,128)} collective-permute-done((f32[16,128]{1,0:T(8,128)}, f32[16,128]{1,0:T(8,128)}, u32[]{:S(2)}, u32[]{:S(2)}) %collective-permute-start.2) | collective-permute-done | bytes 8224 | tf_op jit(solution)/shard_map/ppermute | solution.py:97
  155.6 0.7 select_add_fusion.2
  156.3 2.1 %collective-permute-start.3 = (f32[8,128]{1,0:T(8,128)S(1)}, f32[8,128]{1,0:T(8,128)S(1)}, u32[]{:S(2)}, u32[]{:S(2)}) collective-permute-start(f32[8,128]{1,0:T(8,128)S(1)} %slice_select_fusion.3), channel_id=1, source_target_pairs={{0,32},{8,40},{16,48},{24,56},{32,0},{40,8},{48,16},{56,24},{64,96... | collective-permute-start | bytes 12296 | tf_op jit(solution)/shard_map/ppermute | solution.py:97
  158.3 3.0 %fusion.30 = (f32[2,4,12,8]{3,1,2,0:T(4,128)}, f32[2,4,12,1,8,4]{4,5,1,2,0,3:T(4,128)}) fusion(bf16[2,4,12,8,128]{4,3,1,2,0:T(8,128)(2,1)S(1)} %reshape.159, bf16[2,4,12,128]{3,1,2,0:T(4,128)(2,1)} %param.15, pred[4,4]{1,0:T(4,128)(4,1)} %iota_compare_fusion.3), kind=kOutput, calls=%fused_computation.65 | convolution fusion | flops 794880 | bytes 236560 | tf_op jit(solution)/shard_map/lsrkgd,ltrkd->lsrkgt/dot_general | solution.py:29
  161.4 1.5 collective-permute-done.3
  162.8 2.2 %collective-permute-start.4 = (f32[4,128]{1,0:T(4,128)S(1)}, f32[4,128]{1,0:T(4,128)S(1)}, u32[]{:S(2)}, u32[]{:S(2)}) collective-permute-start(f32[4,128]{1,0:T(4,128)S(1)} %slice_select_fusion.4), channel_id=1, source_target_pairs={{0,16},{8,24},{16,0},{24,8},{32,48},{40,56},{48,32},{56,40},{64,80... | collective-permute-start | bytes 6152 | tf_op jit(solution)/shard_map/ppermute | solution.py:97
  165.1 2.2 %fusion.29 = (f32[2,4,12,8]{3,1,2,0:T(4,128)}, f32[2,4,12,1,8,128]{5,4,1,2,0,3:T(8,128)S(1)}) fusion(bf16[2,4,12,8,128]{4,3,1,2,0:T(8,128)(2,1)} %copy-done.2, bf16[2,12,128,128]{3,2,1,0:T(8,128)(2,1)S(1)} %copy-done.1), kind=kOutput, calls=%fused_computation.64 | convolution fusion | flops 25361664 | bytes 1379328 | tf_op jit(solution)/shard_map/lsrkgd,lrckd->lsrkgc/dot_general | solution.py:25
  167.2 0.8 max.8
  168.1 0.3 collective-permute-done.4
  168.3 1.9 collective-permute-start.5
  170.3 0.4 fusion.9
  170.6 0.7 collective-permute-done.5
  171.4 3.3 %collective-permute-start.6 = (f32[2,128]{1,0:T(2,128)S(1)}, f32[2,128]{1,0:T(2,128)S(1)}, u32[]{:S(2)}, u32[]{:S(2)}) collective-permute-start(f32[2,128]{1,0:T(2,128)S(1)} %select_add_fusion.5), channel_id=1, source_target_pairs={{0,1},{1,0},{2,3},{3,2},{4,5},{5,4},{6,7},{7,6},{8,9},{9,8},{10,11... | collective-permute-start | bytes 3080 | tf_op jit(solution)/shard_map/ppermute | solution.py:103
  174.7 1.1 fusion.13
  175.9 2.5 %collective-permute-done.6 = f32[2,128]{1,0:T(2,128)S(1)} collective-permute-done((f32[2,128]{1,0:T(2,128)S(1)}, f32[2,128]{1,0:T(2,128)S(1)}, u32[]{:S(2)}, u32[]{:S(2)}) %collective-permute-start.6) | collective-permute-done | bytes 1056 | tf_op jit(solution)/shard_map/ppermute | solution.py:103
  178.3 2.8 %collective-permute-start.7 = (f32[2,128]{1,0:T(2,128)S(1)}, f32[2,128]{1,0:T(2,128)S(1)}, u32[]{:S(2)}, u32[]{:S(2)}) collective-permute-start(f32[2,128]{1,0:T(2,128)S(1)} %add.136), channel_id=1, source_target_pairs={{0,2},{1,3},{2,0},{3,1},{4,6},{5,7},{6,4},{7,5},{8,10},{9,11},{10,... | collective-permute-start | bytes 3080 | tf_op jit(solution)/shard_map/ppermute | solution.py:103
  181.1 1.5 fusion.6
  182.6 1.3 collective-permute-done.7
  183.9 3.1 %collective-permute-start.8 = (f32[2,128]{1,0:T(2,128)S(1)}, f32[2,128]{1,0:T(2,128)S(1)}, u32[]{:S(2)}, u32[]{:S(2)}) collective-permute-start(f32[2,128]{1,0:T(2,128)S(1)} %add.137), channel_id=1, source_target_pairs={{0,4},{1,5},{2,6},{3,7},{4,0},{5,1},{6,2},{7,3},{8,12},{9,13},{10,... | collective-permute-start | bytes 3080 | tf_op jit(solution)/shard_map/ppermute | solution.py:103
  187.1 0.3 fusion.2
  187.4 0.7 reshape.162
  188.2 2.7 %collective-permute-done.8 = f32[2,128]{1,0:T(2,128)S(1)} collective-permute-done((f32[2,128]{1,0:T(2,128)S(1)}, f32[2,128]{1,0:T(2,128)S(1)}, u32[]{:S(2)}, u32[]{:S(2)}) %collective-permute-start.8) | collective-permute-done | bytes 1056 | tf_op jit(solution)/shard_map/ppermute | solution.py:103
  190.9 0.6 add.138
  191.4 1.0 copy.24
  (36 shorter events, 0.1 us)
Async XLA Ops:
  0.6 5.3 %copy-start = (bf16[80,2,2,16,128]{4,3,2,1,0:T(8,128)(2,1)S(1)}, bf16[80,2,2,16,128]{4,3,2,1,0:T(8,128)(2,1)}, u32[]{:S(2)}) copy-start(bf16[80,2,2,16,128]{4,3,2,1,0:T(8,128)(2,1)} %param.17) | copy-start | bytes 3932164
  8.6 18.1 %copy-start.8 = (s32[64]{0:T(128)S(1)}, s32[64]{0:T(128)}, u32[]{:S(2)}) copy-start(s32[64]{0:T(128)} %param.19) | copy-start | bytes 772
  8.6 18.1 %copy-start.9 = (s32[64]{0:T(128)S(1)}, s32[64]{0:T(128)}, u32[]{:S(2)}) copy-start(s32[64]{0:T(128)} %param.20) | copy-start | bytes 772
  8.6 18.2 %copy-start.6 = (bf16[2,2,128,128]{3,2,1,0:T(8,128)(2,1)S(1)}, bf16[2,2,128,128]{3,2,1,0:T(8,128)(2,1)}, u32[]{:S(2)}) copy-start(bf16[2,2,128,128]{3,2,1,0:T(8,128)(2,1)} %param.23) | copy-start | bytes 393220
  8.6 69.4 %all-to-all-start = ((bf16[64,2,2,16,128]{4,3,2,1,0:T(8,128)(2,1)}), bf16[64,2,2,16,128]{4,3,2,1,0:T(8,128)(2,1)S(1)}, u32[]{:S(2)}, u32[]{:S(2)}) async-start(bf16[64,2,2,16,128]{4,3,2,1,0:T(8,128)(2,1)} %broadcast_select_fusion), calls=%async_computation | async-start | bytes 2097152 | tf_op jit(solution)/shard_map/all_to_all | solution.py:82
  79.7 68.6 %copy-start.3 = (bf16[2,4,12,1024]{3,1,2,0:T(4,128)(2,1)S(1)}, bf16[2,4,12,1024]{3,1,2,0:T(4,128)(2,1)}, u32[]{:S(2)}) copy-start(bf16[2,4,12,1024]{3,1,2,0:T(4,128)(2,1)} %param.12) | copy-start | bytes 589828
  79.7 111.8 %all-to-all-start.1 = ((bf16[64,2,2,16,128]{4,3,2,1,0:T(8,128)(2,1)}), bf16[64,2,2,16,128]{4,3,2,1,0:T(8,128)(2,1)S(1)}, u32[]{:S(2)}, u32[]{:S(2)}) async-start(bf16[64,2,2,16,128]{4,3,2,1,0:T(8,128)(2,1)} %gather_fusion.1), calls=%async_computation.1 | async-start | bytes 2097152 | tf_op jit(solution)/shard_map/all_to_all | solution.py:110
  87.8 77.3 %copy-start.1 = (bf16[2,12,128,128]{3,2,1,0:T(8,128)(2,1)S(1)}, bf16[2,12,128,128]{3,2,1,0:T(8,128)(2,1)}, u32[]{:S(2)}) copy-start(bf16[2,12,128,128]{3,2,1,0:T(8,128)(2,1)} %param.13) | copy-start | bytes 2359300
  88.0 6.3 %collective-permute-start = (f32[64,128]{1,0:T(8,128)S(1)}, f32[64,128]{1,0:T(8,128)S(1)}, u32[]{:S(2)}, u32[]{:S(2)}) collective-permute-start(f32[64,128]{1,0:T(8,128)S(1)} %slice_select_fusion), channel_id=1, source_target_pairs={{0,256},{8,264},{16,272},{24,280},{32,288},{40,296},{48,304},{56,3... | collective-permute-start | bytes 98312 | tf_op jit(solution)/shard_map/ppermute | solution.py:97
  94.3 50.9 %collective-permute-start.1 = (f32[32,128]{1,0:T(8,128)S(1)}, f32[32,128]{1,0:T(8,128)S(1)}, u32[]{:S(2)}, u32[]{:S(2)}) collective-permute-start(f32[32,128]{1,0:T(8,128)S(1)} %slice_select_fusion.1), channel_id=1, source_target_pairs={{0,128},{8,136},{16,144},{24,152},{32,160},{40,168},{48,176},{56,1... | collective-permute-start | bytes 49160 | tf_op jit(solution)/shard_map/ppermute | solution.py:97
  145.8 9.8 %collective-permute-start.2 = (f32[16,128]{1,0:T(8,128)}, f32[16,128]{1,0:T(8,128)}, u32[]{:S(2)}, u32[]{:S(2)}) collective-permute-start(f32[16,128]{1,0:T(8,128)} %slice_select_fusion.2), channel_id=1, source_target_pairs={{0,64},{8,72},{16,80},{24,88},{32,96},{40,104},{48,112},{56,120},{... | collective-permute-start | bytes 24584 | tf_op jit(solution)/shard_map/ppermute | solution.py:97
  148.3 14.5 %copy-start.2 = (bf16[2,4,12,8,128]{4,3,1,2,0:T(8,128)(2,1)}, bf16[2,4,12,8,128]{4,3,1,2,0:T(8,128)(2,1)S(1)}, u32[]{:S(2)}) copy-start(bf16[2,4,12,8,128]{4,3,1,2,0:T(8,128)(2,1)S(1)} %reshape.159) | copy-start | bytes 589828
  156.3 18.4 %copy-start.5 = (pred[4,4]{1,0:T(4,128)(4,1)S(1)}, pred[4,4]{1,0:T(4,128)(4,1)}, u32[]{:S(2)}) copy-start(pred[4,4]{1,0:T(4,128)(4,1)} %iota_compare_fusion.3) | copy-start | bytes 52
  156.3 6.5 %collective-permute-start.3 = (f32[8,128]{1,0:T(8,128)S(1)}, f32[8,128]{1,0:T(8,128)S(1)}, u32[]{:S(2)}, u32[]{:S(2)}) collective-permute-start(f32[8,128]{1,0:T(8,128)S(1)} %slice_select_fusion.3), channel_id=1, source_target_pairs={{0,32},{8,40},{16,48},{24,56},{32,0},{40,8},{48,16},{56,24},{64,96... | collective-permute-start | bytes 12296 | tf_op jit(solution)/shard_map/ppermute | solution.py:97
  162.8 5.5 %collective-permute-start.4 = (f32[4,128]{1,0:T(4,128)S(1)}, f32[4,128]{1,0:T(4,128)S(1)}, u32[]{:S(2)}, u32[]{:S(2)}) collective-permute-start(f32[4,128]{1,0:T(4,128)S(1)} %slice_select_fusion.4), channel_id=1, source_target_pairs={{0,16},{8,24},{16,0},{24,8},{32,48},{40,56},{48,32},{56,40},{64,80... | collective-permute-start | bytes 6152 | tf_op jit(solution)/shard_map/ppermute | solution.py:97
  168.3 3.0 %collective-permute-start.5 = (f32[2,128]{1,0:T(2,128)S(1)}, f32[2,128]{1,0:T(2,128)S(1)}, u32[]{:S(2)}, u32[]{:S(2)}) collective-permute-start(f32[2,128]{1,0:T(2,128)S(1)} %broadcast_select_fusion.1), channel_id=1, source_target_pairs={{0,8},{8,0},{16,24},{24,16},{32,40},{40,32},{48,56},{56,48},{64,72... | collective-permute-start | bytes 3080 | tf_op jit(solution)/shard_map/ppermute | solution.py:97
  171.4 7.0 %collective-permute-start.6 = (f32[2,128]{1,0:T(2,128)S(1)}, f32[2,128]{1,0:T(2,128)S(1)}, u32[]{:S(2)}, u32[]{:S(2)}) collective-permute-start(f32[2,128]{1,0:T(2,128)S(1)} %select_add_fusion.5), channel_id=1, source_target_pairs={{0,1},{1,0},{2,3},{3,2},{4,5},{5,4},{6,7},{7,6},{8,9},{9,8},{10,11... | collective-permute-start | bytes 3080 | tf_op jit(solution)/shard_map/ppermute | solution.py:103
  178.3 8.7 %copy-start.4 = (f32[2,4,12,1,8,4]{4,5,1,2,0,3:T(4,128)S(1)}, f32[2,4,12,1,8,4]{4,5,1,2,0,3:T(4,128)}, u32[]{:S(2)}) copy-start(f32[2,4,12,1,8,4]{4,5,1,2,0,3:T(4,128)} %get-tuple-element.6) | copy-start | bytes 36868
  178.3 8.7 %copy-start.7 = (bf16[2,4,12,128]{3,1,2,0:T(4,128)(2,1)S(1)}, bf16[2,4,12,128]{3,1,2,0:T(4,128)(2,1)}, u32[]{:S(2)}) copy-start(bf16[2,4,12,128]{3,1,2,0:T(4,128)(2,1)} %param.16) | copy-start | bytes 73732
  178.3 5.6 %collective-permute-start.7 = (f32[2,128]{1,0:T(2,128)S(1)}, f32[2,128]{1,0:T(2,128)S(1)}, u32[]{:S(2)}, u32[]{:S(2)}) collective-permute-start(f32[2,128]{1,0:T(2,128)S(1)} %add.136), channel_id=1, source_target_pairs={{0,2},{1,3},{2,0},{3,1},{4,6},{5,7},{6,4},{7,5},{8,10},{9,11},{10,... | collective-permute-start | bytes 3080 | tf_op jit(solution)/shard_map/ppermute | solution.py:103
  183.9 7.0 %collective-permute-start.8 = (f32[2,128]{1,0:T(2,128)S(1)}, f32[2,128]{1,0:T(2,128)S(1)}, u32[]{:S(2)}, u32[]{:S(2)}) collective-permute-start(f32[2,128]{1,0:T(2,128)S(1)} %add.137), channel_id=1, source_target_pairs={{0,4},{1,5},{2,6},{3,7},{4,0},{5,1},{6,2},{7,3},{8,12},{9,13},{10,... | collective-permute-start | bytes 3080 | tf_op jit(solution)/shard_map/ppermute | solution.py:103

commit v3 on v1

--- a/solution.py
+++ b/solution.py
@@ -3,6 +3,8 @@
 import jax
 import jax.numpy as jnp
 from jax import lax
+from jax.experimental import pallas as pl
+from jax.experimental.pallas import tpu as pltpu
 from jax.sharding import PartitionSpec as P
 
 HD = 128
@@ -49,6 +51,114 @@
         "lsrkgt,ltrkd->lsrkgd", new_weights, fresh_values, preferred_element_type=jnp.float32
     )
     return mixed.astype(jnp.bfloat16).reshape(layers, steps, requests, qwidth)
+
+
+def take_kernel(source_ref, length_ref, list_ref, pool_ref, own_ref, out_ref):
+    place = lax.axis_index("inst")
+    step = pl.program_id(0)
+    rows, span = out_ref.shape[0], out_ref.shape[3]
+
+    @pl.when(step == 0)
+    def _():
+        def find(i, found):
+            return jnp.where(source_ref[i] == place, i, found)
+
+        own_ref[0] = lax.fori_loop(0, source_ref.shape[0], find, jnp.int32(0), unroll=8)
+
+    own = own_ref[0]
+    length = length_ref[own]
+
+    def take(b, carry):
+        first = (step * rows + b) * span
+        slot = list_ref[own, step * rows + b]
+        block = pool_ref[slot]
+        token = first + lax.broadcasted_iota(jnp.int32, block.shape, 2)
+        out_ref[b] = jnp.where(token < length, block.astype(jnp.float32), 0.0).astype(block.dtype)
+        return carry
+
+    lax.fori_loop(0, rows, take, 0, unroll=4)
+
+
+def take_blocks(mig_source, mig_lengths, block_lists, kv_pool):
+    depth = block_lists.shape[1]
+    rows = depth // 4
+    smem = pl.BlockSpec(memory_space=pltpu.SMEM)
+    return pl.pallas_call(
+        take_kernel,
+        grid=(depth // rows,),
+        in_specs=[smem, smem, smem, pl.BlockSpec(memory_space=pltpu.VMEM)],
+        out_specs=[
+            pl.BlockSpec(memory_space=pltpu.SMEM),
+            pl.BlockSpec((rows,) + kv_pool.shape[1:], lambda i: (i, 0, 0, 0, 0)),
+        ],
+        out_shape=[
+            jax.ShapeDtypeStruct((1,), jnp.int32),
+            jax.ShapeDtypeStruct((depth,) + kv_pool.shape[1:], kv_pool.dtype),
+        ],
+        compiler_params=pltpu.CompilerParams(vmem_limit_bytes=16 * 1024 * 1024),
+    )(mig_source, mig_lengths, block_lists, kv_pool)
+
+
+def relay_kernel(source_ref, target_ref, held_ref, terms_ref, out_ref, sems):
+    pieces = held_ref.shape[1]
+    whole = out_ref.at[:, pl.ds(0, pieces)]
+    rest = pltpu.make_async_copy(terms_ref, out_ref.at[:, pl.ds(pieces, 1)], sems.at[1])
+    rest.start()
+
+    def send(r, carry):
+        pltpu.make_async_copy(
+            held_ref.at[source_ref[r]],
+            out_ref.at[target_ref[r], pl.ds(0, pieces)],
+            sems.at[0],
+        ).start()
+        return carry
+
+    lax.fori_loop(0, source_ref.shape[0], send, 0, unroll=8)
+    pltpu.make_async_copy(held_ref, whole, sems.at[0]).wait()
+    rest.wait()
+
+
+def order_by_target(mig_source, mig_target, held, terms):
+    smem = pl.BlockSpec(memory_space=pltpu.SMEM)
+    anywhere = pl.BlockSpec(memory_space=pl.ANY)
+    return pl.pallas_call(
+        relay_kernel,
+        in_specs=[smem, smem, anywhere, anywhere],
+        out_specs=anywhere,
+        out_shape=jax.ShapeDtypeStruct(
+            (held.shape[0], held.shape[1] + 1) + held.shape[2:], held.dtype
+        ),
+        scratch_shapes=[pltpu.SemaphoreType.DMA((2,))],
+    )(mig_source, mig_target, held, terms)
+
+
+def split_kernel(landed_ref, arrived_ref, sums_ref, terms, sems):
+    pieces = arrived_ref.shape[1]
+    blocks = pltpu.make_async_copy(landed_ref.at[:, pl.ds(0, pieces)], arrived_ref, sems.at[0])
+    blocks.start()
+    rest = pltpu.make_async_copy(landed_ref.at[:, pl.ds(pieces, 1)], terms, sems.at[1])
+    rest.start()
+    rest.wait()
+    sums_ref[...] = jnp.sum(terms[:, 0].astype(jnp.float32), axis=0)
+    blocks.wait()
+
+
+def split_landed(landed):
+    members, pieces, slots, width = landed.shape
+    anywhere = pl.BlockSpec(memory_space=pl.ANY)
+    return pl.pallas_call(
+        split_kernel,
+        in_specs=[anywhere],
+        out_specs=[anywhere, pl.BlockSpec(memory_space=pltpu.VMEM)],
+        out_shape=[
+            jax.ShapeDtypeStruct((members, pieces - 1, slots, width), landed.dtype),
+            jax.ShapeDtypeStruct((slots, width), jnp.float32),
+        ],
+        scratch_shapes=[
+            pltpu.VMEM((members, 1, slots, width), landed.dtype),
+            pltpu.SemaphoreType.DMA((2,)),
+        ],
+    )(landed)
 
 
 def local(
@@ -68,17 +178,9 @@
     attention = decode_attention(queries, cache_keys, cache_values, new_keys, new_values)
     members = lax.axis_size("inst")
     heads = lax.axis_size("tp")
-    place = lax.axis_index("inst")
-    request_ids = jnp.arange(mig_source.shape[0], dtype=jnp.int32)
-    own_request = jnp.sum(jnp.where(mig_source == place, request_ids, 0))
-    length = mig_lengths[own_request]
-    slot_row = block_lists[own_request]
-    blocks = kv_pool[slot_row]
-    depth, layers, pair, span, width = blocks.shape
-    position = jnp.arange(depth)[:, None] * span + jnp.arange(span)[None, :]
-    blocks = jnp.where(
-        (position < length)[:, None, None, :, None], blocks, jnp.zeros((), blocks.dtype)
-    )
+    own_request, blocks = take_blocks(mig_source, mig_lengths, block_lists, kv_pool)
+    own_request = own_request[0]
+    width = blocks.shape[-1]
     sectioned = lax.all_to_all(blocks, "inst", split_axis=0, concat_axis=0, tiled=True)
 
     projected = jnp.einsum("blktd,lkde->blkte", blocks, check_key, preferred_element_type=jnp.float32)
@@ -93,15 +195,12 @@
         reach *= 2
     terms = table.astype(jnp.bfloat16).reshape(members, 1, SLOTS, table.shape[-1])
 
-    source_of = jnp.sum(
-        jnp.where(mig_target[None, :] == request_ids[:, None], mig_source[None, :], 0), axis=1
-    )
-    onward = sectioned[source_of].reshape(members, -1, SLOTS, width)
-    landed = lax.all_to_all(
-        jnp.concatenate([onward, terms], axis=1), "inst", split_axis=0, concat_axis=0, tiled=True
-    )
-    arrived = landed[:, :-1].reshape(blocks.shape)
-    checksums = jnp.sum(landed[:, -1].astype(jnp.float32), axis=0)
+    onward = order_by_target(
+        mig_source, mig_target, sectioned.reshape(members, -1, SLOTS, width), terms
+    )
+    landed = lax.all_to_all(onward, "inst", split_axis=0, concat_axis=0, tiled=True)
+    arrived, checksums = split_landed(landed)
+    arrived = arrived.reshape(blocks.shape)
     return (attention, arrived, checksums)
 
 

time: 148 us -> 211 us (1.43)
  Pallas kernels: 0 us -> 70.9 us
  other arithmetic: 7.81 us -> 1.27 us
    pallas_call x0 -> x3, Pallas kernels: none -> 70.9 us  [the longest x1 34.5 us: order_by_target(): pl.pallas_call(relay_kernel, in_specs=[smem, smem, anywhere, anywhere], o...]
    unnamed x16 -> x24, local copies, waits for them, and re-layouts: 0.37 us -> 5.77 us
    all_to_all x1, waiting for transfers between devices: 32.7 us -> 29.9 us  [local(): lax.all_to_all(blocks, 'inst', split_axis=0, concat_axis=0, tiled=True)]
    concatenate x1 -> x0, other arithmetic: 2.39 us -> none  [local(): jnp.concatenate([onward, terms], axis=1)]
    reduce_sum x3 -> x0, other arithmetic: 2.14 us -> none  [the longest x1 1.39 us: local(): own_request = jnp.sum(jnp.where(mig_source == place, request_ids, 0))]
    slice x1 -> x0, local copies, waits for them, and re-layouts: 2.13 us -> none  [local(): arrived = landed[:, :-1].reshape(blocks.shape)]
  transfers between devices with their start and end apart: 5 -> 5, of which waited for: 5 -> 5; matrix products, arithmetic and copies ran while one was open for 5% -> 3% of each run, Pallas kernels for 0% -> 0%
where the time goes in v3:
time: 211 us; the launch traced here: 210 us
  waiting for transfers between devices  91.1 us (43%)
  Pallas kernels  70.9 us (34%)
  starting transfers between devices  32.5 us (15%)
  local copies, waits for them, and re-layouts  7.27 us (3%)
  matrix products  4.21 us (2%)
  between operations  2.77 us (1%)
    all_to_all x1, waiting for transfers between devices, local(): lax.all_to_all(onward, 'inst', split_axis=0, concat_axis=0, tiled=True)  51.5 us
    pallas_call x1, Pallas kernels, order_by_target(): pl.pallas_call(relay_kernel, in_specs=[smem, smem, anywhere, anywhere], o...  34.5 us
    pallas_call x1, Pallas kernels, split_landed(): pl.pallas_call(split_kernel, in_specs=[anywhere], out_specs=[anywhere, pl...  33.4 us
    all_to_all x1, waiting for transfers between devices, local(): lax.all_to_all(blocks, 'inst', split_axis=0, concat_axis=0, tiled=True)  29.9 us
    all_to_all x1, starting transfers between devices, local(): lax.all_to_all(blocks, 'inst', split_axis=0, concat_axis=0, tiled=True)  17.1 us
    ppermute x3, waiting for transfers between devices, local(): lax.ppermute(table, 'tp', [(i, i ^ reach) for i in range(heads)])  9.69 us
    ppermute x3, starting transfers between devices, local(): lax.ppermute(table, 'tp', [(i, i ^ reach) for i in range(heads)])  9.6 us
    all_to_all x1, starting transfers between devices, local(): lax.all_to_all(onward, 'inst', split_axis=0, concat_axis=0, tiled=True)  5.8 us
  transfers between devices with their start and end apart: 5, of which 5 were waited for; matrix products, arithmetic and copies ran while one was open for 3% of the time, Pallas kernels for 0%

profile of v3, /device:TPU:57, one launch (start us, length us, event | category | flops | bytes accessed | tf_op | source)
XLA Modules:
  0.0 210.0 jit_solution(17752661825966210071)
XLA Ops:
  0.6 0.0 copy-start
  0.6 0.0 copy-start.1
  0.7 1.4 copy-done.1
  2.0 0.0 copy-start.2
  2.0 0.8 copy-done.2
  2.8 0.0 copy-start.3
  2.8 0.7 copy-done.3
  3.5 0.0 copy-start.4
  3.5 0.7 copy-done.4
  4.1 2.9 %shard_map.139 = (s32[1]{0:T(128)}, bf16[64,2,2,16,128]{4,3,2,1,0:T(8,128)(2,1)}) custom-call(s32[64]{0:T(128)S(1)} %copy-done.3, s32[64]{0:T(128)S(1)} %copy-done.4, s32[64,64]{1,0:T(8,128)S(1)} %copy-done.2, bf16[80,2,2,16,128]{4,3,2,1,0:T(8,128)(2,1)S(1)} %copy-done.1), custom_call_target="tpu_custom_call" | custom-call | tf_op jit(solution)/shard_map/pallas_call | solution.py:86
  7.0 0.0 copy-start.9
  7.0 17.1 %all-to-all-start = ((bf16[64,2,2,16,128]{4,3,2,1,0:T(8,128)(2,1)}), bf16[64,2,2,16,128]{4,3,2,1,0:T(8,128)(2,1)S(1)}, u32[]{:S(2)}, u32[]{:S(2)}) async-start(bf16[64,2,2,16,128]{4,3,2,1,0:T(8,128)(2,1)} %get-tuple-element.7), calls=%async_computation | async-start | bytes 2097152 | tf_op jit(solution)/shard_map/all_to_all | solution.py:184
  26.1 0.7 dynamic-slice_bitcast_fusion
  26.8 0.0 copy-done.9
  26.8 1.7 tanh_reduce_fusion
  28.5 0.2 fusion.18
  28.7 4.4 %collective-permute-start = (f32[128,128]{1,0:T(8,128)S(1)}, f32[128,128]{1,0:T(8,128)S(1)}, u32[]{:S(2)}, u32[]{:S(2)}) collective-permute-start(f32[128,128]{1,0:T(8,128)S(1)} %fusion.18), channel_id=1, source_target_pairs={{0,1},{1,0},{2,3},{3,2},{4,5},{5,4},{6,7},{7,6},{8,9},{9,8},{10,11... | collective-permute-start | bytes 196616 | tf_op jit(solution)/shard_map/ppermute | solution.py:194
  33.0 2.8 %collective-permute-done = f32[128,128]{1,0:T(8,128)S(1)} collective-permute-done((f32[128,128]{1,0:T(8,128)S(1)}, f32[128,128]{1,0:T(8,128)S(1)}, u32[]{:S(2)}, u32[]{:S(2)}) %collective-permute-start) | collective-permute-done | bytes 65568 | tf_op jit(solution)/shard_map/ppermute | solution.py:194
  35.9 2.4 %collective-permute-start.1 = (f32[128,128]{1,0:T(8,128)S(1)}, f32[128,128]{1,0:T(8,128)S(1)}, u32[]{:S(2)}, u32[]{:S(2)}) collective-permute-start(f32[128,128]{1,0:T(8,128)S(1)} %add.29), channel_id=1, source_target_pairs={{0,2},{1,3},{2,0},{3,1},{4,6},{5,7},{6,4},{7,5},{8,10},{9,11},{10,... | collective-permute-start | bytes 196616 | tf_op jit(solution)/shard_map/ppermute | solution.py:194
  38.3 2.9 %collective-permute-done.1 = f32[128,128]{1,0:T(8,128)S(1)} collective-permute-done((f32[128,128]{1,0:T(8,128)S(1)}, f32[128,128]{1,0:T(8,128)S(1)}, u32[]{:S(2)}, u32[]{:S(2)}) %collective-permute-start.1) | collective-permute-done | bytes 65568 | tf_op jit(solution)/shard_map/ppermute | solution.py:194
  41.2 2.9 %collective-permute-start.2 = (f32[128,128]{1,0:T(8,128)S(1)}, f32[128,128]{1,0:T(8,128)S(1)}, u32[]{:S(2)}, u32[]{:S(2)}) collective-permute-start(f32[128,128]{1,0:T(8,128)S(1)} %add.30), channel_id=1, source_target_pairs={{0,4},{1,5},{2,6},{3,7},{4,0},{5,1},{6,2},{7,3},{8,12},{9,13},{10,... | collective-permute-start | bytes 196616 | tf_op jit(solution)/shard_map/ppermute | solution.py:194
  44.1 3.9 %collective-permute-done.2 = f32[128,128]{1,0:T(8,128)S(1)} collective-permute-done((f32[128,128]{1,0:T(8,128)S(1)}, f32[128,128]{1,0:T(8,128)S(1)}, u32[]{:S(2)}, u32[]{:S(2)}) %collective-permute-start.2) | collective-permute-done | bytes 65568 | tf_op jit(solution)/shard_map/ppermute | solution.py:194
  48.0 0.6 add_convert_fusion
  48.7 29.9 %all-to-all-done = bf16[64,2,2,16,128]{4,3,2,1,0:T(8,128)(2,1)S(1)} async-done(((bf16[64,2,2,16,128]{4,3,2,1,0:T(8,128)(2,1)}), bf16[64,2,2,16,128]{4,3,2,1,0:T(8,128)(2,1)S(1)}, u32[]{:S(2)}, u32[]{:S(2)}) %all-to-all-start) | async-done | bytes 1048608 | tf_op jit(solution)/shard_map/all_to_all | solution.py:184
  78.5 0.0 copy-start.6
  78.5 1.0 copy-done.6
  79.5 34.5 %shard_map.140 = bf16[64,33,2,128]{3,2,1,0:T(2,128)(2,1)} custom-call(s32[64]{0:T(128)} %source_ref.3, s32[64]{0:T(128)} %target_ref.1, bf16[64,32,2,128]{3,2,1,0:T(2,128)(2,1)} %bitcast.65, bf16[64,1,2,128]{3,2,1,0:T(2,128)(2,1)} %bitcast.66), custom_call_target="tpu_custom_call" | custom-call | tf_op jit(solution)/shard_map/pallas_call | solution.py:124
  114.0 0.0 copy-start.7
  114.1 5.8 %all-to-all-start.1 = ((bf16[64,33,2,128]{3,2,1,0:T(2,128)(2,1)}), bf16[64,33,2,128]{3,2,1,0:T(2,128)(2,1)S(1)}, u32[]{:S(2)}, u32[]{:S(2)}) async-start(bf16[64,33,2,128]{3,2,1,0:T(2,128)(2,1)} %shard_map.140), calls=%async_computation.1 | async-start | bytes 2162688 | tf_op jit(solution)/shard_map/all_to_all | solution.py:201
  119.9 0.0 copy-done.7
  119.9 0.0 copy-start.10
  119.9 0.1 reshape.99
  120.0 0.0 copy-done
  120.0 0.0 copy-start.8
  120.0 0.6 fusion.26
  120.6 0.0 copy-done.10
  120.6 1.0 fusion.27
  121.6 0.2 fusion.13
  121.9 0.4 fusion.9
  122.3 0.0 copy-done.8
  122.3 0.0 copy-start.11
  122.3 0.4 fusion.6
  122.7 0.3 copy-done.11
  123.0 0.3 fusion.2
  123.4 0.7 reshape.102
  124.1 51.5 %all-to-all-done.1.landed_ref = bf16[64,33,2,128]{3,2,1,0:T(2,128)(2,1)S(1)} async-done(((bf16[64,33,2,128]{3,2,1,0:T(2,128)(2,1)}), bf16[64,33,2,128]{3,2,1,0:T(2,128)(2,1)S(1)}, u32[]{:S(2)}, u32[]{:S(2)}) %all-to-all-start.1) | async-done | bytes 1081376 | tf_op jit(solution)/shard_map/all_to_all | solution.py:201
  175.6 1.0 copy-done.5
  176.6 33.4 %shard_map.141 = (bf16[64,32,2,128]{3,2,1,0:T(2,128)(2,1)}, f32[2,128]{1,0:T(2,128)}) custom-call(bf16[64,33,2,128]{3,2,1,0:T(2,128)(2,1)} %copy-done.5), custom_call_target="tpu_custom_call" | custom-call | tf_op jit(solution)/shard_map/pallas_call | solution.py:149
  (6 shorter events, 0.1 us)
Async XLA Ops:
  0.6 119.3 %copy-start = (bf16[2,12,128,128]{3,2,1,0:T(8,128)(2,1)S(1)}, bf16[2,12,128,128]{3,2,1,0:T(8,128)(2,1)}, u32[]{:S(2)}) copy-start(bf16[2,12,128,128]{3,2,1,0:T(8,128)(2,1)} %param.13) | copy-start | bytes 2359300
  0.6 1.4 copy-start.1
  2.0 0.8 copy-start.2
  2.8 0.7 copy-start.3
  3.5 0.7 copy-start.4
  7.0 19.8 %copy-start.9 = (bf16[2,2,128,128]{3,2,1,0:T(8,128)(2,1)S(1)}, bf16[2,2,128,128]{3,2,1,0:T(8,128)(2,1)}, u32[]{:S(2)}) copy-start(bf16[2,2,128,128]{3,2,1,0:T(8,128)(2,1)} %param.23) | copy-start | bytes 393220
  7.0 71.5 %all-to-all-start = ((bf16[64,2,2,16,128]{4,3,2,1,0:T(8,128)(2,1)}), bf16[64,2,2,16,128]{4,3,2,1,0:T(8,128)(2,1)S(1)}, u32[]{:S(2)}, u32[]{:S(2)}) async-start(bf16[64,2,2,16,128]{4,3,2,1,0:T(8,128)(2,1)} %get-tuple-element.7), calls=%async_computation | async-start | bytes 2097152 | tf_op jit(solution)/shard_map/all_to_all | solution.py:184
  28.7 7.2 %collective-permute-start = (f32[128,128]{1,0:T(8,128)S(1)}, f32[128,128]{1,0:T(8,128)S(1)}, u32[]{:S(2)}, u32[]{:S(2)}) collective-permute-start(f32[128,128]{1,0:T(8,128)S(1)} %fusion.18), channel_id=1, source_target_pairs={{0,1},{1,0},{2,3},{3,2},{4,5},{5,4},{6,7},{7,6},{8,9},{9,8},{10,11... | collective-permute-start | bytes 196616 | tf_op jit(solution)/shard_map/ppermute | solution.py:194
  35.9 5.3 %collective-permute-start.1 = (f32[128,128]{1,0:T(8,128)S(1)}, f32[128,128]{1,0:T(8,128)S(1)}, u32[]{:S(2)}, u32[]{:S(2)}) collective-permute-start(f32[128,128]{1,0:T(8,128)S(1)} %add.29), channel_id=1, source_target_pairs={{0,2},{1,3},{2,0},{3,1},{4,6},{5,7},{6,4},{7,5},{8,10},{9,11},{10,... | collective-permute-start | bytes 196616 | tf_op jit(solution)/shard_map/ppermute | solution.py:194
  41.2 6.8 %collective-permute-start.2 = (f32[128,128]{1,0:T(8,128)S(1)}, f32[128,128]{1,0:T(8,128)S(1)}, u32[]{:S(2)}, u32[]{:S(2)}) collective-permute-start(f32[128,128]{1,0:T(8,128)S(1)} %add.30), channel_id=1, source_target_pairs={{0,4},{1,5},{2,6},{3,7},{4,0},{5,1},{6,2},{7,3},{8,12},{9,13},{10,... | collective-permute-start | bytes 196616 | tf_op jit(solution)/shard_map/ppermute | solution.py:194
  78.5 1.0 copy-start.6
  114.0 5.8 %copy-start.7 = (bf16[2,4,12,1024]{3,1,2,0:T(4,128)(2,1)S(1)}, bf16[2,4,12,1024]{3,1,2,0:T(4,128)(2,1)}, u32[]{:S(2)}) copy-start(bf16[2,4,12,1024]{3,1,2,0:T(4,128)(2,1)} %param.12) | copy-start | bytes 589828
  114.1 61.5 %all-to-all-start.1 = ((bf16[64,33,2,128]{3,2,1,0:T(2,128)(2,1)}), bf16[64,33,2,128]{3,2,1,0:T(2,128)(2,1)S(1)}, u32[]{:S(2)}, u32[]{:S(2)}) async-start(bf16[64,33,2,128]{3,2,1,0:T(2,128)(2,1)} %shard_map.140), calls=%async_computation.1 | async-start | bytes 2162688 | tf_op jit(solution)/shard_map/all_to_all | solution.py:201
  119.9 0.8 copy-start.10
  120.0 2.3 %copy-start.8 = (bf16[2,12,128,128]{3,2,1,0:T(8,128)(2,1)S(1)}, bf16[2,12,128,128]{3,2,1,0:T(8,128)(2,1)}, u32[]{:S(2)}) copy-start(bf16[2,12,128,128]{3,2,1,0:T(8,128)(2,1)} %param.14) | copy-start | bytes 2359300
  122.3 0.7 copy-start.11
  175.6 1.0 copy-start.5

commit v4 on v1

--- a/solution.py
+++ b/solution.py
@@ -3,6 +3,8 @@
 import jax
 import jax.numpy as jnp
 from jax import lax
+from jax.experimental import pallas as pl
+from jax.experimental.pallas import tpu as pltpu
 from jax.sharding import PartitionSpec as P
 
 HD = 128
@@ -51,6 +53,72 @@
     return mixed.astype(jnp.bfloat16).reshape(layers, steps, requests, qwidth)
 
 
+def take_kernel(
+    source_hbm, length_hbm, list_hbm, pool_hbm, own_ref, out_hbm, source, lengths, lists, pool, stage, sems
+):
+    fetches = [
+        pltpu.make_async_copy(*pair, sems.at[n])
+        for n, pair in enumerate(
+            [(source_hbm, source), (length_hbm, lengths), (list_hbm, lists), (pool_hbm, pool)]
+        )
+    ]
+    for fetch in fetches:
+        fetch.start()
+    place = lax.axis_index("inst")
+    depth, span = stage.shape[0], stage.shape[3]
+    rows = depth // 4
+    fetches[0].wait()
+    own = jnp.int32(0)
+    for i in range(source.shape[0]):
+        own = jnp.where(source[i] == place, jnp.int32(i), own)
+    own_ref[0] = own
+    for fetch in fetches[1:]:
+        fetch.wait()
+    length = lengths[own]
+
+    def clear(b, carry):
+        block = stage[b]
+        token = b * span + lax.broadcasted_iota(jnp.int32, block.shape, 2)
+        stage[b] = jnp.where(token < length, block.astype(jnp.float32), 0.0).astype(block.dtype)
+        return carry
+
+    writes = []
+    for n in range(depth // rows):
+        for b in range(n * rows, (n + 1) * rows):
+            stage[b] = pool[lists[own, b]]
+        lax.fori_loop(jnp.maximum(length // span, n * rows), (n + 1) * rows, clear, 0)
+        part = pl.ds(n * rows, rows)
+        writes.append(pltpu.make_async_copy(stage.at[part], out_hbm.at[part], sems.at[4 + n]))
+        writes[-1].start()
+    for write in writes:
+        write.wait()
+
+
+def take_blocks(mig_source, mig_lengths, block_lists, kv_pool):
+    depth = block_lists.shape[1]
+    return pl.pallas_call(
+        take_kernel,
+        in_specs=[pl.BlockSpec(memory_space=pltpu.HBM)] * 4,
+        out_specs=[
+            pl.BlockSpec(memory_space=pltpu.SMEM),
+            pl.BlockSpec(memory_space=pltpu.HBM),
+        ],
+        out_shape=[
+            jax.ShapeDtypeStruct((1,), jnp.int32),
+            jax.ShapeDtypeStruct((depth,) + kv_pool.shape[1:], kv_pool.dtype),
+        ],
+        scratch_shapes=[
+            pltpu.SMEM(mig_source.shape, jnp.int32),
+            pltpu.SMEM(mig_lengths.shape, jnp.int32),
+            pltpu.SMEM(block_lists.shape, jnp.int32),
+            pltpu.VMEM(kv_pool.shape, kv_pool.dtype),
+            pltpu.VMEM((depth,) + kv_pool.shape[1:], kv_pool.dtype),
+            pltpu.SemaphoreType.DMA((8,)),
+        ],
+        compiler_params=pltpu.CompilerParams(vmem_limit_bytes=60 * 1024 * 1024),
+    )(mig_source, mig_lengths, block_lists, kv_pool)
+
+
 def local(
     queries,
     cache_keys,
@@ -68,17 +136,10 @@
     attention = decode_attention(queries, cache_keys, cache_values, new_keys, new_values)
     members = lax.axis_size("inst")
     heads = lax.axis_size("tp")
-    place = lax.axis_index("inst")
     request_ids = jnp.arange(mig_source.shape[0], dtype=jnp.int32)
-    own_request = jnp.sum(jnp.where(mig_source == place, request_ids, 0))
-    length = mig_lengths[own_request]
-    slot_row = block_lists[own_request]
-    blocks = kv_pool[slot_row]
-    depth, layers, pair, span, width = blocks.shape
-    position = jnp.arange(depth)[:, None] * span + jnp.arange(span)[None, :]
-    blocks = jnp.where(
-        (position < length)[:, None, None, :, None], blocks, jnp.zeros((), blocks.dtype)
-    )
+    own_request, blocks = take_blocks(mig_source, mig_lengths, block_lists, kv_pool)
+    own_request = own_request[0]
+    width = blocks.shape[-1]
     sectioned = lax.all_to_all(blocks, "inst", split_axis=0, concat_axis=0, tiled=True)
 
     projected = jnp.einsum("blktd,lkde->blkte", blocks, check_key, preferred_element_type=jnp.float32)

time: 148 us -> 143 us (0.966)
  other arithmetic: 7.81 us -> 3.8 us
  Pallas kernels: 0 us -> 2.96 us
  local copies, waits for them, and re-layouts: 7.68 us -> 4.77 us
    pallas_call x0 -> x1, Pallas kernels: none -> 2.96 us  [take_blocks(): pl.pallas_call(take_kernel, in_specs=[pl.BlockSpec(memory_space=pltpu.HBM...]
    select_n x2 -> x0, other arithmetic: 1.88 us -> none  [the longest x1 1.18 us: local(): jnp.where((position < length)[:, None, None, :, None], blocks, jnp.zeros(...]
    all_to_all x1, waiting for transfers between devices: 32.7 us -> 30.9 us  [local(): lax.all_to_all(blocks, 'inst', split_axis=0, concat_axis=0, tiled=True)]
  transfers between devices with their start and end apart: 5 -> 5, of which waited for: 5 -> 5; matrix products, arithmetic and copies ran while one was open for 5% -> 4% of each run, Pallas kernels for 0% -> 0%
where the time goes in v4:
time: 143 us
  waiting for transfers between devices  92.7 us (65%)
  starting transfers between devices  32.5 us (23%)
  local copies, waits for them, and re-layouts  4.77 us (3%)
  other arithmetic  3.8 us (3%)
  matrix products  2.98 us (2%)
  Pallas kernels  2.96 us (2%)
  between operations  2.82 us (2%)
    all_to_all x1, waiting for transfers between devices, local(): lax.all_to_all(jnp.concatenate([onward, terms], axis=1), 'inst', split_ax...  51.5 us
    all_to_all x1, waiting for transfers between devices, local(): lax.all_to_all(blocks, 'inst', split_axis=0, concat_axis=0, tiled=True)  30.9 us
    all_to_all x1, starting transfers between devices, local(): lax.all_to_all(blocks, 'inst', split_axis=0, concat_axis=0, tiled=True)  17.1 us
    ppermute x3, waiting for transfers between devices, local(): lax.ppermute(table, 'tp', [(i, i ^ reach) for i in range(heads)])  10.4 us
    ppermute x3, starting transfers between devices, local(): lax.ppermute(table, 'tp', [(i, i ^ reach) for i in range(heads)])  9.59 us
    all_to_all x1, starting transfers between devices, local(): lax.all_to_all(jnp.concatenate([onward, terms], axis=1), 'inst', split_ax...  5.79 us
    pallas_call x1, Pallas kernels, take_blocks(): pl.pallas_call(take_kernel, in_specs=[pl.BlockSpec(memory_space=pltpu.HBM...  2.96 us
  transfers between devices with their start and end apart: 5, of which 5 were waited for; matrix products, arithmetic and copies ran while one was open for 4% of the time, Pallas kernels for 0%

profile of v4, /device:TPU:57, one launch (start us, length us, event | category | flops | bytes accessed | tf_op | source)
XLA Modules:
  0.0 142.6 jit_solution(14566587685862253990)
XLA Ops:
  0.6 0.0 copy-start
  0.6 3.0 %shard_map.139 = (s32[1]{0:T(128)}, bf16[64,2,2,16,128]{4,3,2,1,0:T(8,128)(2,1)}) custom-call(s32[64]{0:T(128)} %source_hbm.1, s32[64]{0:T(128)} %length_hbm.1, s32[64,64]{1,0:T(8,128)} %list_hbm.1, bf16[80,2,2,16,128]{4,3,2,1,0:T(8,128)(2,1)} %pool_hbm.1), custom_call_target="tpu_custom_call" | custom-call | tf_op jit(solution)/shard_map/pallas_call | solution.py:99
  3.6 0.0 copy-start.1
  3.6 0.0 copy-start.5
  3.6 17.1 %all-to-all-start = ((bf16[64,2,2,16,128]{4,3,2,1,0:T(8,128)(2,1)}), bf16[64,2,2,16,128]{4,3,2,1,0:T(8,128)(2,1)S(1)}, u32[]{:S(2)}, u32[]{:S(2)}) async-start(bf16[64,2,2,16,128]{4,3,2,1,0:T(8,128)(2,1)} %get-tuple-element.5), calls=%async_computation | async-start | bytes 2097152 | tf_op jit(solution)/shard_map/all_to_all | solution.py:143
  22.7 0.7 dynamic-slice_bitcast_fusion
  23.4 0.0 copy-done.1
  23.4 0.0 copy-done.5
  23.4 0.0 copy-start.3
  23.4 0.0 copy-start.8
  23.4 0.5 tanh_reduce_fusion
  23.9 0.2 fusion.18
  24.1 4.4 %collective-permute-start = (f32[128,128]{1,0:T(8,128)S(1)}, f32[128,128]{1,0:T(8,128)S(1)}, u32[]{:S(2)}, u32[]{:S(2)}) collective-permute-start(f32[128,128]{1,0:T(8,128)S(1)} %fusion.18), channel_id=1, source_target_pairs={{0,1},{1,0},{2,3},{3,2},{4,5},{5,4},{6,7},{7,6},{8,9},{9,8},{10,11... | collective-permute-start | bytes 196616 | tf_op jit(solution)/shard_map/ppermute | solution.py:153
  28.5 0.0 copy-done.3
  28.5 0.0 copy-done.8
  28.5 0.1 select_reduce_fusion
  28.6 3.5 %collective-permute-done = f32[128,128]{1,0:T(8,128)S(1)} collective-permute-done((f32[128,128]{1,0:T(8,128)S(1)}, f32[128,128]{1,0:T(8,128)S(1)}, u32[]{:S(2)}, u32[]{:S(2)}) %collective-permute-start) | collective-permute-done | bytes 65568 | tf_op jit(solution)/shard_map/ppermute | solution.py:153
  32.1 2.4 %collective-permute-start.1 = (f32[128,128]{1,0:T(8,128)S(1)}, f32[128,128]{1,0:T(8,128)S(1)}, u32[]{:S(2)}, u32[]{:S(2)}) collective-permute-start(f32[128,128]{1,0:T(8,128)S(1)} %add.44), channel_id=1, source_target_pairs={{0,2},{1,3},{2,0},{3,1},{4,6},{5,7},{6,4},{7,5},{8,10},{9,11},{10,... | collective-permute-start | bytes 196616 | tf_op jit(solution)/shard_map/ppermute | solution.py:153
  34.5 2.9 %collective-permute-done.1 = f32[128,128]{1,0:T(8,128)S(1)} collective-permute-done((f32[128,128]{1,0:T(8,128)S(1)}, f32[128,128]{1,0:T(8,128)S(1)}, u32[]{:S(2)}, u32[]{:S(2)}) %collective-permute-start.1) | collective-permute-done | bytes 65568 | tf_op jit(solution)/shard_map/ppermute | solution.py:153
  37.4 2.9 %collective-permute-start.2 = (f32[128,128]{1,0:T(8,128)S(1)}, f32[128,128]{1,0:T(8,128)S(1)}, u32[]{:S(2)}, u32[]{:S(2)}) collective-permute-start(f32[128,128]{1,0:T(8,128)S(1)} %add.45), channel_id=1, source_target_pairs={{0,4},{1,5},{2,6},{3,7},{4,0},{5,1},{6,2},{7,3},{8,12},{9,13},{10,... | collective-permute-start | bytes 196616 | tf_op jit(solution)/shard_map/ppermute | solution.py:153
  40.3 3.9 %collective-permute-done.2 = f32[128,128]{1,0:T(8,128)S(1)} collective-permute-done((f32[128,128]{1,0:T(8,128)S(1)}, f32[128,128]{1,0:T(8,128)S(1)}, u32[]{:S(2)}, u32[]{:S(2)}) %collective-permute-start.2) | collective-permute-done | bytes 65568 | tf_op jit(solution)/shard_map/ppermute | solution.py:153
  44.3 30.9 %all-to-all-done = bf16[64,2,2,16,128]{4,3,2,1,0:T(8,128)(2,1)S(1)} async-done(((bf16[64,2,2,16,128]{4,3,2,1,0:T(8,128)(2,1)}), bf16[64,2,2,16,128]{4,3,2,1,0:T(8,128)(2,1)S(1)}, u32[]{:S(2)}, u32[]{:S(2)}) %all-to-all-start) | async-done | bytes 1048608 | tf_op jit(solution)/shard_map/all_to_all | solution.py:143
  75.1 0.7 gather_fusion
  75.9 2.4 %pad_maximum_fusion = bf16[64,33,2,128]{3,2,1,0:T(2,128)(2,1)} fusion(bf16[64,1,2,128]{3,2,1,0:T(2,128)(2,1)S(1)} %bitcast.73, bf16[64,32,2,128]{3,2,1,0:T(2,128)(2,1)S(1)} %bitcast.71), kind=kLoop, calls=%fused_computation.10 | loop fusion | flops 540672 | bytes 2162688 | tf_op jit(solution)/shard_map/concatenate | solution.py:162
  78.3 0.0 copy-start.2
  78.3 5.8 %all-to-all-start.1 = ((bf16[64,33,2,128]{3,2,1,0:T(2,128)(2,1)}), bf16[64,33,2,128]{3,2,1,0:T(2,128)(2,1)S(1)}, u32[]{:S(2)}, u32[]{:S(2)}) async-start(bf16[64,33,2,128]{3,2,1,0:T(2,128)(2,1)} %pad_maximum_fusion), calls=%async_computation.1 | async-start | bytes 2162688 | tf_op jit(solution)/shard_map/all_to_all | solution.py:161
  84.1 0.0 copy-done.2
  84.1 0.0 copy-start.6
  84.1 0.1 reshape.115
  84.2 0.0 copy-done
  84.2 0.6 fusion.27
  84.8 0.0 copy-done.6
  84.8 0.0 copy-start.4
  84.8 1.0 fusion.28
  85.9 0.2 fusion.13
  86.1 0.4 fusion.9
  86.5 0.0 copy-done.4
  86.5 0.0 copy-start.7
  86.5 0.4 fusion.6
  86.9 0.3 copy-done.7
  87.2 0.3 fusion.2
  87.6 0.7 reshape.118
  88.3 51.5 %all-to-all-done.1 = bf16[64,33,2,128]{3,2,1,0:T(2,128)(2,1)S(1)} async-done(((bf16[64,33,2,128]{3,2,1,0:T(2,128)(2,1)}), bf16[64,33,2,128]{3,2,1,0:T(2,128)(2,1)S(1)}, u32[]{:S(2)}, u32[]{:S(2)}) %all-to-all-start.1) | async-done | bytes 1081376 | tf_op jit(solution)/shard_map/all_to_all | solution.py:161
  139.8 2.1 %slice.10 = bf16[64,32,2,128]{3,2,1,0:T(2,128)(2,1)} slice(bf16[64,33,2,128]{3,2,1,0:T(2,128)(2,1)S(1)} %all-to-all-done.1), slice={[0:64], [0:32], [0:2], [0:128]} | slice | bytes 2097152 | tf_op jit(solution)/shard_map/slice | solution.py:164
  141.9 0.6 convert_reduce_fusion
  (8 shorter events, 0.1 us)
Async XLA Ops:
  0.6 83.6 %copy-start = (bf16[2,12,128,128]{3,2,1,0:T(8,128)(2,1)S(1)}, bf16[2,12,128,128]{3,2,1,0:T(8,128)(2,1)}, u32[]{:S(2)}) copy-start(bf16[2,12,128,128]{3,2,1,0:T(8,128)(2,1)} %param.13) | copy-start | bytes 2359300
  3.6 19.8 %copy-start.1 = (bf16[64,2,2,16,128]{4,3,2,1,0:T(8,128)(2,1)S(1)}, bf16[64,2,2,16,128]{4,3,2,1,0:T(8,128)(2,1)}, u32[]{:S(2)}) copy-start(bf16[64,2,2,16,128]{4,3,2,1,0:T(8,128)(2,1)} %get-tuple-element.5) | copy-start | bytes 3145732
  3.6 19.8 %copy-start.5 = (bf16[2,2,128,128]{3,2,1,0:T(8,128)(2,1)S(1)}, bf16[2,2,128,128]{3,2,1,0:T(8,128)(2,1)}, u32[]{:S(2)}) copy-start(bf16[2,2,128,128]{3,2,1,0:T(8,128)(2,1)} %param.23) | copy-start | bytes 393220
  3.6 71.5 %all-to-all-start = ((bf16[64,2,2,16,128]{4,3,2,1,0:T(8,128)(2,1)}), bf16[64,2,2,16,128]{4,3,2,1,0:T(8,128)(2,1)S(1)}, u32[]{:S(2)}, u32[]{:S(2)}) async-start(bf16[64,2,2,16,128]{4,3,2,1,0:T(8,128)(2,1)} %get-tuple-element.5), calls=%async_computation | async-start | bytes 2097152 | tf_op jit(solution)/shard_map/all_to_all | solution.py:143
  23.4 5.0 %copy-start.3 = (s32[64]{0:T(128)S(1)}, s32[64]{0:T(128)}, u32[]{:S(2)}) copy-start(s32[64]{0:T(128)} %source_hbm.1) | copy-start | bytes 772
  23.4 5.0 %copy-start.8 = (s32[64]{0:T(128)S(1)}, s32[64]{0:T(128)}, u32[]{:S(2)}) copy-start(s32[64]{0:T(128)} %param.20) | copy-start | bytes 772
  24.1 8.0 %collective-permute-start = (f32[128,128]{1,0:T(8,128)S(1)}, f32[128,128]{1,0:T(8,128)S(1)}, u32[]{:S(2)}, u32[]{:S(2)}) collective-permute-start(f32[128,128]{1,0:T(8,128)S(1)} %fusion.18), channel_id=1, source_target_pairs={{0,1},{1,0},{2,3},{3,2},{4,5},{5,4},{6,7},{7,6},{8,9},{9,8},{10,11... | collective-permute-start | bytes 196616 | tf_op jit(solution)/shard_map/ppermute | solution.py:153
  32.1 5.3 %collective-permute-start.1 = (f32[128,128]{1,0:T(8,128)S(1)}, f32[128,128]{1,0:T(8,128)S(1)}, u32[]{:S(2)}, u32[]{:S(2)}) collective-permute-start(f32[128,128]{1,0:T(8,128)S(1)} %add.44), channel_id=1, source_target_pairs={{0,2},{1,3},{2,0},{3,1},{4,6},{5,7},{6,4},{7,5},{8,10},{9,11},{10,... | collective-permute-start | bytes 196616 | tf_op jit(solution)/shard_map/ppermute | solution.py:153
  37.4 6.8 %collective-permute-start.2 = (f32[128,128]{1,0:T(8,128)S(1)}, f32[128,128]{1,0:T(8,128)S(1)}, u32[]{:S(2)}, u32[]{:S(2)}) collective-permute-start(f32[128,128]{1,0:T(8,128)S(1)} %add.45), channel_id=1, source_target_pairs={{0,4},{1,5},{2,6},{3,7},{4,0},{5,1},{6,2},{7,3},{8,12},{9,13},{10,... | collective-permute-start | bytes 196616 | tf_op jit(solution)/shard_map/ppermute | solution.py:153
  78.3 5.8 %copy-start.2 = (bf16[2,4,12,1024]{3,1,2,0:T(4,128)(2,1)S(1)}, bf16[2,4,12,1024]{3,1,2,0:T(4,128)(2,1)}, u32[]{:S(2)}) copy-start(bf16[2,4,12,1024]{3,1,2,0:T(4,128)(2,1)} %param.12) | copy-start | bytes 589828
  78.3 61.5 %all-to-all-start.1 = ((bf16[64,33,2,128]{3,2,1,0:T(2,128)(2,1)}), bf16[64,33,2,128]{3,2,1,0:T(2,128)(2,1)S(1)}, u32[]{:S(2)}, u32[]{:S(2)}) async-start(bf16[64,33,2,128]{3,2,1,0:T(2,128)(2,1)} %pad_maximum_fusion), calls=%async_computation.1 | async-start | bytes 2162688 | tf_op jit(solution)/shard_map/all_to_all | solution.py:161
  84.1 0.7 copy-start.6
  84.8 1.6 %copy-start.4 = (bf16[2,12,128,128]{3,2,1,0:T(8,128)(2,1)S(1)}, bf16[2,12,128,128]{3,2,1,0:T(8,128)(2,1)}, u32[]{:S(2)}) copy-start(bf16[2,12,128,128]{3,2,1,0:T(8,128)(2,1)} %param.14) | copy-start | bytes 2359300
  86.5 0.7 copy-start.7

commit v5 on v4

--- a/solution.py
+++ b/solution.py
@@ -119,6 +119,79 @@
     )(mig_source, mig_lengths, block_lists, kv_pool)
 
 
+def relay_kernel(source_ref, target_ref, held_ref, terms_ref, out_ref, source_of):
+    depth = held_ref.shape[0]
+    rows = held_ref.shape[1]
+    group = 8
+
+    terms = terms_ref[...]
+    for r in range(depth):
+        source_of[target_ref[r]] = source_ref[r]
+    for first in range(0, depth, group):
+        pieces = []
+        for t in range(first, first + group):
+            pieces.append(held_ref[source_of[t]])
+            pieces.append(terms[t * SLOTS : (t + 1) * SLOTS])
+        size = (rows + SLOTS) * group
+        whole = jnp.concatenate(pieces, axis=0)
+        out_ref[pl.ds(first * (rows + SLOTS), size)] = whole.astype(out_ref.dtype)
+
+
+def order_by_target(mig_source, mig_target, held, terms):
+    smem = pl.BlockSpec(memory_space=pltpu.SMEM)
+    vmem = pl.BlockSpec(memory_space=pltpu.VMEM)
+    return pl.pallas_call(
+        relay_kernel,
+        in_specs=[smem, smem, vmem, vmem],
+        out_specs=vmem,
+        out_shape=jax.ShapeDtypeStruct(
+            (held.shape[0] * (held.shape[1] + SLOTS), held.shape[2]), held.dtype
+        ),
+        scratch_shapes=[pltpu.SMEM(mig_target.shape, jnp.int32)],
+        compiler_params=pltpu.CompilerParams(vmem_limit_bytes=16 * 1024 * 1024),
+    )(mig_source, mig_target, held, terms)
+
+
+def split_kernel(landed_ref, arrived_hbm, sums_ref, stage, sems):
+    depth, rows = stage.shape[:2]
+    group = 8
+    total = jnp.zeros(sums_ref.shape, jnp.float32)
+    writes = []
+    for first in range(0, depth, group):
+        size = (rows + SLOTS) * group
+        whole = landed_ref[pl.ds(first * (rows + SLOTS), size)]
+        for j in range(group):
+            base = j * (rows + SLOTS)
+            stage[first + j] = whole[base : base + rows].astype(stage.dtype)
+            total = total + whole[base + rows : base + rows + SLOTS].astype(jnp.float32)
+        part = pl.ds(first, group)
+        writes.append(pltpu.make_async_copy(stage.at[part], arrived_hbm.at[part], sems.at[first // group]))
+        writes[-1].start()
+    sums_ref[...] = total
+    for write in writes:
+        write.wait()
+
+
+def split_landed(landed, depth):
+    rows = landed.shape[0] // depth - SLOTS
+    width = landed.shape[1]
+    vmem = pl.BlockSpec(memory_space=pltpu.VMEM)
+    return pl.pallas_call(
+        split_kernel,
+        in_specs=[vmem],
+        out_specs=[pl.BlockSpec(memory_space=pl.ANY), vmem],
+        out_shape=[
+            jax.ShapeDtypeStruct((depth, rows, width), landed.dtype),
+            jax.ShapeDtypeStruct((SLOTS, width), jnp.float32),
+        ],
+        scratch_shapes=[
+            pltpu.VMEM((depth, rows, width), landed.dtype),
+            pltpu.SemaphoreType.DMA((depth // 8,)),
+        ],
+        compiler_params=pltpu.CompilerParams(vmem_limit_bytes=16 * 1024 * 1024),
+    )(landed)
+
+
 def local(
     queries,
     cache_keys,
@@ -136,7 +209,6 @@
     attention = decode_attention(queries, cache_keys, cache_values, new_keys, new_values)
     members = lax.axis_size("inst")
     heads = lax.axis_size("tp")
-    request_ids = jnp.arange(mig_source.shape[0], dtype=jnp.int32)
     own_request, blocks = take_blocks(mig_source, mig_lengths, block_lists, kv_pool)
     own_request = own_request[0]
     width = blocks.shape[-1]
@@ -152,17 +224,14 @@
     while reach < heads:
         table = table + lax.ppermute(table, "tp", [(i, i ^ reach) for i in range(heads)])
         reach *= 2
-    terms = table.astype(jnp.bfloat16).reshape(members, 1, SLOTS, table.shape[-1])
-
-    source_of = jnp.sum(
-        jnp.where(mig_target[None, :] == request_ids[:, None], mig_source[None, :], 0), axis=1
-    )
-    onward = sectioned[source_of].reshape(members, -1, SLOTS, width)
+    terms = table.astype(jnp.bfloat16)
+
+    onward = order_by_target(mig_source, mig_target, sectioned.reshape(members, -1, width), terms)
     landed = lax.all_to_all(
-        jnp.concatenate([onward, terms], axis=1), "inst", split_axis=0, concat_axis=0, tiled=True
-    )
-    arrived = landed[:, :-1].reshape(blocks.shape)
-    checksums = jnp.sum(landed[:, -1].astype(jnp.float32), axis=0)
+        onward.reshape(members, -1, SLOTS, width), "inst", split_axis=0, concat_axis=0, tiled=True
+    )
+    arrived, checksums = split_landed(landed.reshape(onward.shape), members)
+    arrived = arrived.reshape(blocks.shape)
     return (attention, arrived, checksums)
 
 

time: 143 us -> 141 us (0.986)
  Pallas kernels: 2.96 us -> 6.44 us
  other arithmetic: 3.8 us -> 0.66 us
  local copies, waits for them, and re-layouts: 4.77 us -> 1.88 us
    pallas_call x0 -> x2, Pallas kernels: none -> 3.38 us  [the longest x1 1.77 us: order_by_target(): pl.pallas_call(relay_kernel, in_specs=[smem, smem, vmem, vmem], out_specs...]
    concatenate x1 -> x0, other arithmetic: 2.39 us -> none  [local(): jnp.concatenate([onward, terms], axis=1)]
    slice x1 -> x0, local copies, waits for them, and re-layouts: 2.13 us -> none  [local(): arrived = landed[:, :-1].reshape(blocks.shape)]
where the time goes in v5:
time: 141 us; the launch traced here: 140 us
  waiting for transfers between devices  92.9 us (66%)
  starting transfers between devices  32.4 us (23%)
  Pallas kernels  6.44 us (5%)
  matrix products  2.98 us (2%)
  between operations  2.78 us (2%)
  local copies, waits for them, and re-layouts  1.88 us (1%)
    all_to_all x1, waiting for transfers between devices, local(): lax.all_to_all(onward.reshape(members, -1, SLOTS, width), 'inst', split_a...  51.5 us
    all_to_all x1, waiting for transfers between devices, local(): lax.all_to_all(blocks, 'inst', split_axis=0, concat_axis=0, tiled=True)  30.9 us
    all_to_all x1, starting transfers between devices, local(): lax.all_to_all(blocks, 'inst', split_axis=0, concat_axis=0, tiled=True)  17 us
    ppermute x3, waiting for transfers between devices, local(): lax.ppermute(table, 'tp', [(i, i ^ reach) for i in range(heads)])  10.5 us
    ppermute x3, starting transfers between devices, local(): lax.ppermute(table, 'tp', [(i, i ^ reach) for i in range(heads)])  9.59 us
    all_to_all x1, starting transfers between devices, local(): lax.all_to_all(onward.reshape(members, -1, SLOTS, width), 'inst', split_a...  5.79 us
    pallas_call x1, Pallas kernels, take_blocks(): pl.pallas_call(take_kernel, in_specs=[pl.BlockSpec(memory_space=pltpu.HBM...  3.05 us
  transfers between devices with their start and end apart: 5, of which 5 were waited for; matrix products, arithmetic and copies ran while one was open for 4% of the time, Pallas kernels for 0%

profile of v5, /device:TPU:57, one launch (start us, length us, event | category | flops | bytes accessed | tf_op | source)
XLA Modules:
  0.0 140.1 jit_solution(16856110870284419869)
XLA Ops:
  0.6 0.0 copy-start
  0.6 3.1 %shard_map.139 = (s32[1]{0:T(128)}, bf16[64,2,2,16,128]{4,3,2,1,0:T(8,128)(2,1)}) custom-call(s32[64]{0:T(128)} %source_ref.1, s32[64]{0:T(128)} %length_hbm.1, s32[64,64]{1,0:T(8,128)} %list_hbm.1, bf16[80,2,2,16,128]{4,3,2,1,0:T(8,128)(2,1)} %pool_hbm.1), custom_call_target="tpu_custom_call" | custom-call | tf_op jit(solution)/shard_map/pallas_call | solution.py:99
  3.7 0.0 copy-start.3
  3.7 0.0 copy-start.6
  3.7 17.0 %all-to-all-start = ((bf16[64,2,2,16,128]{4,3,2,1,0:T(8,128)(2,1)}), bf16[64,2,2,16,128]{4,3,2,1,0:T(8,128)(2,1)S(1)}, u32[]{:S(2)}, u32[]{:S(2)}) async-start(bf16[64,2,2,16,128]{4,3,2,1,0:T(8,128)(2,1)} %get-tuple-element.7), calls=%async_computation | async-start | bytes 2097152 | tf_op jit(solution)/shard_map/all_to_all | solution.py:215
  22.7 0.7 dynamic-slice_bitcast_fusion
  23.4 0.0 copy-done.3
  23.4 0.0 copy-done.6
  23.4 0.0 copy-start.1
  23.4 0.0 copy-start.2
  23.4 0.5 tanh_reduce_fusion
  23.9 0.2 fusion.18
  24.1 4.4 %collective-permute-start = (f32[128,128]{1,0:T(8,128)S(1)}, f32[128,128]{1,0:T(8,128)S(1)}, u32[]{:S(2)}, u32[]{:S(2)}) collective-permute-start(f32[128,128]{1,0:T(8,128)S(1)} %fusion.18), channel_id=1, source_target_pairs={{0,1},{1,0},{2,3},{3,2},{4,5},{5,4},{6,7},{7,6},{8,9},{9,8},{10,11... | collective-permute-start | bytes 196616 | tf_op jit(solution)/shard_map/ppermute | solution.py:225
  28.5 3.7 %collective-permute-done = f32[128,128]{1,0:T(8,128)S(1)} collective-permute-done((f32[128,128]{1,0:T(8,128)S(1)}, f32[128,128]{1,0:T(8,128)S(1)}, u32[]{:S(2)}, u32[]{:S(2)}) %collective-permute-start) | collective-permute-done | bytes 65568 | tf_op jit(solution)/shard_map/ppermute | solution.py:225
  32.1 2.4 %collective-permute-start.1 = (f32[128,128]{1,0:T(8,128)S(1)}, f32[128,128]{1,0:T(8,128)S(1)}, u32[]{:S(2)}, u32[]{:S(2)}) collective-permute-start(f32[128,128]{1,0:T(8,128)S(1)} %add.29), channel_id=1, source_target_pairs={{0,2},{1,3},{2,0},{3,1},{4,6},{5,7},{6,4},{7,5},{8,10},{9,11},{10,... | collective-permute-start | bytes 196616 | tf_op jit(solution)/shard_map/ppermute | solution.py:225
  34.5 2.9 %collective-permute-done.1 = f32[128,128]{1,0:T(8,128)S(1)} collective-permute-done((f32[128,128]{1,0:T(8,128)S(1)}, f32[128,128]{1,0:T(8,128)S(1)}, u32[]{:S(2)}, u32[]{:S(2)}) %collective-permute-start.1) | collective-permute-done | bytes 65568 | tf_op jit(solution)/shard_map/ppermute | solution.py:225
  37.4 2.9 %collective-permute-start.2 = (f32[128,128]{1,0:T(8,128)S(1)}, f32[128,128]{1,0:T(8,128)S(1)}, u32[]{:S(2)}, u32[]{:S(2)}) collective-permute-start(f32[128,128]{1,0:T(8,128)S(1)} %add.30), channel_id=1, source_target_pairs={{0,4},{1,5},{2,6},{3,7},{4,0},{5,1},{6,2},{7,3},{8,12},{9,13},{10,... | collective-permute-start | bytes 196616 | tf_op jit(solution)/shard_map/ppermute | solution.py:225
  40.3 3.9 %collective-permute-done.2 = f32[128,128]{1,0:T(8,128)S(1)} collective-permute-done((f32[128,128]{1,0:T(8,128)S(1)}, f32[128,128]{1,0:T(8,128)S(1)}, u32[]{:S(2)}, u32[]{:S(2)}) %collective-permute-start.2) | collective-permute-done | bytes 65568 | tf_op jit(solution)/shard_map/ppermute | solution.py:225
  44.3 30.9 %all-to-all-done = bf16[64,2,2,16,128]{4,3,2,1,0:T(8,128)(2,1)S(1)} async-done(((bf16[64,2,2,16,128]{4,3,2,1,0:T(8,128)(2,1)}), bf16[64,2,2,16,128]{4,3,2,1,0:T(8,128)(2,1)S(1)}, u32[]{:S(2)}, u32[]{:S(2)}) %all-to-all-start) | async-done | bytes 1048608 | tf_op jit(solution)/shard_map/all_to_all | solution.py:215
  75.1 0.0 copy-done.1
  75.1 0.0 copy-done.2
  75.1 1.8 %shard_map.140 = bf16[4224,128]{1,0:T(8,128)(2,1)} custom-call(s32[64]{0:T(128)S(1)} %copy-done.1, s32[64]{0:T(128)S(1)} %copy-done.2, bf16[64,64,128]{2,1,0:T(8,128)(2,1)S(1)} %bitcast.67, bf16[128,128]{1,0:T(8,128)(2,1)S(1)} %add_convert_fusion.terms_ref), custom_call_target="tpu_custom_call" | custom-call | tf_op jit(solution)/shard_map/pallas_call | solution.py:143
  76.9 0.0 copy-start.4
  76.9 5.8 %all-to-all-start.1 = ((bf16[64,33,2,128]{3,2,1,0:T(2,128)(2,1)}), bf16[64,33,2,128]{3,2,1,0:T(2,128)(2,1)S(1)}, u32[]{:S(2)}, u32[]{:S(2)}) async-start(bf16[64,33,2,128]{3,2,1,0:T(2,128)(2,1)} %bitcast.23), calls=%async_computation.1 | async-start | bytes 2162688 | tf_op jit(solution)/shard_map/all_to_all | solution.py:230
  82.7 0.0 copy-done.4
  82.7 0.0 copy-start.7
  82.7 0.1 reshape.102
  82.8 0.0 copy-done
  82.8 0.0 copy-start.5
  82.8 0.6 fusion.26
  83.5 0.0 copy-done.7
  83.5 1.0 fusion.27
  84.5 0.2 fusion.13
  84.7 0.4 fusion.9
  85.1 0.0 copy-done.5
  85.1 0.0 copy-start.8
  85.1 0.4 fusion.6
  85.5 0.3 copy-done.8
  85.8 0.3 fusion.2
  86.2 0.7 reshape.105
  86.9 51.5 %all-to-all-done.1 = bf16[64,33,2,128]{3,2,1,0:T(2,128)(2,1)S(1)} async-done(((bf16[64,33,2,128]{3,2,1,0:T(2,128)(2,1)}), bf16[64,33,2,128]{3,2,1,0:T(2,128)(2,1)S(1)}, u32[]{:S(2)}, u32[]{:S(2)}) %all-to-all-start.1) | async-done | bytes 1081376 | tf_op jit(solution)/shard_map/all_to_all | solution.py:230
  138.4 1.6 %shard_map.141 = (bf16[64,64,128]{2,1,0:T(8,128)(2,1)}, f32[2,128]{1,0:T(2,128)}) custom-call(bf16[4224,128]{1,0:T(8,128)(2,1)S(1)} %bitcast.66), custom_call_target="tpu_custom_call" | custom-call | tf_op jit(solution)/shard_map/pallas_call | solution.py:179
  (6 shorter events, 0.1 us)
Async XLA Ops:
  0.6 82.2 %copy-start = (bf16[2,12,128,128]{3,2,1,0:T(8,128)(2,1)S(1)}, bf16[2,12,128,128]{3,2,1,0:T(8,128)(2,1)}, u32[]{:S(2)}) copy-start(bf16[2,12,128,128]{3,2,1,0:T(8,128)(2,1)} %param.13) | copy-start | bytes 2359300
  3.7 19.7 %copy-start.3 = (bf16[64,2,2,16,128]{4,3,2,1,0:T(8,128)(2,1)S(1)}, bf16[64,2,2,16,128]{4,3,2,1,0:T(8,128)(2,1)}, u32[]{:S(2)}) copy-start(bf16[64,2,2,16,128]{4,3,2,1,0:T(8,128)(2,1)} %get-tuple-element.7) | copy-start | bytes 3145732
  3.7 19.7 %copy-start.6 = (bf16[2,2,128,128]{3,2,1,0:T(8,128)(2,1)S(1)}, bf16[2,2,128,128]{3,2,1,0:T(8,128)(2,1)}, u32[]{:S(2)}) copy-start(bf16[2,2,128,128]{3,2,1,0:T(8,128)(2,1)} %param.23) | copy-start | bytes 393220
  3.7 71.4 %all-to-all-start = ((bf16[64,2,2,16,128]{4,3,2,1,0:T(8,128)(2,1)}), bf16[64,2,2,16,128]{4,3,2,1,0:T(8,128)(2,1)S(1)}, u32[]{:S(2)}, u32[]{:S(2)}) async-start(bf16[64,2,2,16,128]{4,3,2,1,0:T(8,128)(2,1)} %get-tuple-element.7), calls=%async_computation | async-start | bytes 2097152 | tf_op jit(solution)/shard_map/all_to_all | solution.py:215
  23.4 51.7 %copy-start.1 = (s32[64]{0:T(128)S(1)}, s32[64]{0:T(128)}, u32[]{:S(2)}) copy-start(s32[64]{0:T(128)} %source_ref.1) | copy-start | bytes 772
  23.4 51.7 %copy-start.2 = (s32[64]{0:T(128)S(1)}, s32[64]{0:T(128)}, u32[]{:S(2)}) copy-start(s32[64]{0:T(128)} %target_ref.1) | copy-start | bytes 772
  24.1 8.0 %collective-permute-start = (f32[128,128]{1,0:T(8,128)S(1)}, f32[128,128]{1,0:T(8,128)S(1)}, u32[]{:S(2)}, u32[]{:S(2)}) collective-permute-start(f32[128,128]{1,0:T(8,128)S(1)} %fusion.18), channel_id=1, source_target_pairs={{0,1},{1,0},{2,3},{3,2},{4,5},{5,4},{6,7},{7,6},{8,9},{9,8},{10,11... | collective-permute-start | bytes 196616 | tf_op jit(solution)/shard_map/ppermute | solution.py:225
  32.1 5.3 %collective-permute-start.1 = (f32[128,128]{1,0:T(8,128)S(1)}, f32[128,128]{1,0:T(8,128)S(1)}, u32[]{:S(2)}, u32[]{:S(2)}) collective-permute-start(f32[128,128]{1,0:T(8,128)S(1)} %add.29), channel_id=1, source_target_pairs={{0,2},{1,3},{2,0},{3,1},{4,6},{5,7},{6,4},{7,5},{8,10},{9,11},{10,... | collective-permute-start | bytes 196616 | tf_op jit(solution)/shard_map/ppermute | solution.py:225
  37.4 6.8 %collective-permute-start.2 = (f32[128,128]{1,0:T(8,128)S(1)}, f32[128,128]{1,0:T(8,128)S(1)}, u32[]{:S(2)}, u32[]{:S(2)}) collective-permute-start(f32[128,128]{1,0:T(8,128)S(1)} %add.30), channel_id=1, source_target_pairs={{0,4},{1,5},{2,6},{3,7},{4,0},{5,1},{6,2},{7,3},{8,12},{9,13},{10,... | collective-permute-start | bytes 196616 | tf_op jit(solution)/shard_map/ppermute | solution.py:225
  76.9 5.8 %copy-start.4 = (bf16[2,4,12,1024]{3,1,2,0:T(4,128)(2,1)S(1)}, bf16[2,4,12,1024]{3,1,2,0:T(4,128)(2,1)}, u32[]{:S(2)}) copy-start(bf16[2,4,12,1024]{3,1,2,0:T(4,128)(2,1)} %param.12) | copy-start | bytes 589828
  76.9 61.5 %all-to-all-start.1 = ((bf16[64,33,2,128]{3,2,1,0:T(2,128)(2,1)}), bf16[64,33,2,128]{3,2,1,0:T(2,128)(2,1)S(1)}, u32[]{:S(2)}, u32[]{:S(2)}) async-start(bf16[64,33,2,128]{3,2,1,0:T(2,128)(2,1)} %bitcast.23), calls=%async_computation.1 | async-start | bytes 2162688 | tf_op jit(solution)/shard_map/all_to_all | solution.py:230
  82.7 0.8 copy-start.7
  82.8 2.3 %copy-start.5 = (bf16[2,12,128,128]{3,2,1,0:T(8,128)(2,1)S(1)}, bf16[2,12,128,128]{3,2,1,0:T(8,128)(2,1)}, u32[]{:S(2)}) copy-start(bf16[2,12,128,128]{3,2,1,0:T(8,128)(2,1)} %param.14) | copy-start | bytes 2359300
  85.1 0.7 copy-start.8

commit v6 on v5

--- a/solution.py
+++ b/solution.py
@@ -226,6 +226,8 @@
         reach *= 2
     terms = table.astype(jnp.bfloat16)
 
+    terms, attention = lax.optimization_barrier((terms, attention))
+
     onward = order_by_target(mig_source, mig_target, sectioned.reshape(members, -1, width), terms)
     landed = lax.all_to_all(
         onward.reshape(members, -1, SLOTS, width), "inst", split_axis=0, concat_axis=0, tiled=True

time: 141 us -> 139 us (0.986)
  blocking collectives: 0 us -> 61.2 us
  waiting for transfers between devices: 92.9 us -> 37.5 us
  starting transfers between devices: 32.4 us -> 26.7 us
    all_to_all x0 -> x1, blocking collectives: none -> 61.2 us  [local(): lax.all_to_all(onward.reshape(members, -1, SLOTS, width), 'inst', split_a...]
    all_to_all x1 -> x0, waiting for transfers between devices: 51.5 us -> none  [local(): lax.all_to_all(onward.reshape(members, -1, SLOTS, width), 'inst', split_a...]
    all_to_all x1 -> x0, starting transfers between devices: 5.79 us -> none  [local(): lax.all_to_all(onward.reshape(members, -1, SLOTS, width), 'inst', split_a...]
    ppermute x3, waiting for transfers between devices: 10.5 us -> 6.62 us  [local(): lax.ppermute(table, 'tp', [(i, i ^ reach) for i in range(heads)])]
  transfers between devices with their start and end apart: 5 -> 4, of which waited for: 5 -> 4; matrix products, arithmetic and copies ran while one was open for 4% -> 4% of each run, Pallas kernels for 0% -> 0%
where the time goes in v6:
time: 139 us
  blocking collectives  61.2 us (44%)
  waiting for transfers between devices  37.5 us (27%)
  starting transfers between devices  26.7 us (19%)
  Pallas kernels  5.52 us (4%)
  matrix products  2.98 us (2%)
  between operations  2.79 us (2%)
  local copies, waits for them, and re-layouts  1.56 us (1%)
    all_to_all x1, blocking collectives, local(): lax.all_to_all(onward.reshape(members, -1, SLOTS, width), 'inst', split_a...  61.2 us
    all_to_all x1, waiting for transfers between devices, local(): lax.all_to_all(blocks, 'inst', split_axis=0, concat_axis=0, tiled=True)  30.8 us
    all_to_all x1, starting transfers between devices, local(): lax.all_to_all(blocks, 'inst', split_axis=0, concat_axis=0, tiled=True)  17.1 us
    ppermute x3, starting transfers between devices, local(): lax.ppermute(table, 'tp', [(i, i ^ reach) for i in range(heads)])  9.6 us
    ppermute x3, waiting for transfers between devices, local(): lax.ppermute(table, 'tp', [(i, i ^ reach) for i in range(heads)])  6.62 us
    pallas_call x1, Pallas kernels, take_blocks(): pl.pallas_call(take_kernel, in_specs=[pl.BlockSpec(memory_space=pltpu.HBM...  3.11 us
  transfers between devices with their start and end apart: 4, of which 4 were waited for; matrix products, arithmetic and copies ran while one was open for 4% of the time, Pallas kernels for 0%

profile of v6, /device:TPU:57, one launch (start us, length us, event | category | flops | bytes accessed | tf_op | source)
XLA Modules:
  0.0 138.9 jit_solution(13906492283414203954)
XLA Ops:
  0.6 0.0 copy-start
  0.6 3.1 %shard_map.139 = (s32[1]{0:T(128)}, bf16[64,2,2,16,128]{4,3,2,1,0:T(8,128)(2,1)}) custom-call(s32[64]{0:T(128)} %source_ref.1, s32[64]{0:T(128)} %length_hbm.1, s32[64,64]{1,0:T(8,128)} %list_hbm.1, bf16[80,2,2,16,128]{4,3,2,1,0:T(8,128)(2,1)} %pool_hbm.1), custom_call_target="tpu_custom_call" | custom-call | tf_op jit(solution)/shard_map/pallas_call | solution.py:99
  3.8 0.0 copy-start.3
  3.8 0.0 copy-start.6
  3.8 17.1 %all-to-all-start = ((bf16[64,2,2,16,128]{4,3,2,1,0:T(8,128)(2,1)}), bf16[64,2,2,16,128]{4,3,2,1,0:T(8,128)(2,1)S(1)}, u32[]{:S(2)}, u32[]{:S(2)}) async-start(bf16[64,2,2,16,128]{4,3,2,1,0:T(8,128)(2,1)} %get-tuple-element.10), calls=%async_computation | async-start | bytes 2097152 | tf_op jit(solution)/shard_map/all_to_all | solution.py:215
  22.9 0.7 dynamic-slice_bitcast_fusion
  23.6 0.0 copy-done.3
  23.6 0.0 copy-done.6
  23.6 0.0 copy-start.4
  23.6 0.5 tanh_reduce_fusion
  24.1 0.0 copy-start.7
  24.1 0.2 fusion.18
  24.2 4.4 %collective-permute-start = (f32[128,128]{1,0:T(8,128)S(1)}, f32[128,128]{1,0:T(8,128)S(1)}, u32[]{:S(2)}, u32[]{:S(2)}) collective-permute-start(f32[128,128]{1,0:T(8,128)S(1)} %fusion.18), channel_id=1, source_target_pairs={{0,1},{1,0},{2,3},{3,2},{4,5},{5,4},{6,7},{7,6},{8,9},{9,8},{10,11... | collective-permute-start | bytes 196616 | tf_op jit(solution)/shard_map/ppermute | solution.py:225
  28.6 0.0 copy-done.4
  28.6 0.1 reshape.102
  28.7 0.0 copy-done
  28.7 0.0 copy-start.5
  28.7 0.6 fusion.26
  29.4 0.0 copy-done.7
  29.4 1.0 fusion.27
  30.4 0.4 fusion.9
  30.8 0.2 fusion.13
  31.0 1.3 collective-permute-done
  32.3 0.0 copy-start.8
  32.3 2.4 %collective-permute-start.1 = (f32[128,128]{1,0:T(8,128)S(1)}, f32[128,128]{1,0:T(8,128)S(1)}, u32[]{:S(2)}, u32[]{:S(2)}) collective-permute-start(f32[128,128]{1,0:T(8,128)S(1)} %add.27), channel_id=1, source_target_pairs={{0,2},{1,3},{2,0},{3,1},{4,6},{5,7},{6,4},{7,5},{8,10},{9,11},{10,... | collective-permute-start | bytes 196616 | tf_op jit(solution)/shard_map/ppermute | solution.py:225
  34.7 0.0 copy-done.5
  34.7 0.4 fusion.6
  35.1 0.0 copy-start.1
  35.1 0.0 copy-start.2
  35.1 2.5 %collective-permute-done.1 = f32[128,128]{1,0:T(8,128)S(1)} collective-permute-done((f32[128,128]{1,0:T(8,128)S(1)}, f32[128,128]{1,0:T(8,128)S(1)}, u32[]{:S(2)}, u32[]{:S(2)}) %collective-permute-start.1) | collective-permute-done | bytes 65568 | tf_op jit(solution)/shard_map/ppermute | solution.py:225
  37.6 2.9 %collective-permute-start.2 = (f32[128,128]{1,0:T(8,128)S(1)}, f32[128,128]{1,0:T(8,128)S(1)}, u32[]{:S(2)}, u32[]{:S(2)}) collective-permute-start(f32[128,128]{1,0:T(8,128)S(1)} %add.28), channel_id=1, source_target_pairs={{0,4},{1,5},{2,6},{3,7},{4,0},{5,1},{6,2},{7,3},{8,12},{9,13},{10,... | collective-permute-start | bytes 196616 | tf_op jit(solution)/shard_map/ppermute | solution.py:225
  40.5 0.0 copy-done.8
  40.5 0.3 fusion.2
  40.8 0.7 reshape.105
  41.6 2.9 %collective-permute-done.2 = f32[128,128]{1,0:T(8,128)S(1)} collective-permute-done((f32[128,128]{1,0:T(8,128)S(1)}, f32[128,128]{1,0:T(8,128)S(1)}, u32[]{:S(2)}, u32[]{:S(2)}) %collective-permute-start.2) | collective-permute-done | bytes 65568 | tf_op jit(solution)/shard_map/ppermute | solution.py:225
  44.4 30.8 %all-to-all-done = bf16[64,2,2,16,128]{4,3,2,1,0:T(8,128)(2,1)S(1)} async-done(((bf16[64,2,2,16,128]{4,3,2,1,0:T(8,128)(2,1)}), bf16[64,2,2,16,128]{4,3,2,1,0:T(8,128)(2,1)S(1)}, u32[]{:S(2)}, u32[]{:S(2)}) %all-to-all-start) | async-done | bytes 1048608 | tf_op jit(solution)/shard_map/all_to_all | solution.py:215
  75.3 0.0 copy-done.1
  75.3 0.0 copy-done.2
  75.3 0.8 shard_map.140
  76.1 61.2 %all_to_all.10 = bf16[64,33,2,128]{3,2,1,0:T(2,128)(2,1)S(1)} all-to-all(bf16[64,33,2,128]{3,2,1,0:T(2,128)(2,1)S(1)} %bitcast.67), channel_id=1, replica_groups=mesh['inst'=64,'tp'=8] {'inst'}, dimensions={0} | all-to-all | bytes 2162688 | tf_op jit(solution)/shard_map/all_to_all | solution.py:232
  137.3 1.6 %shard_map.141 = (bf16[64,64,128]{2,1,0:T(8,128)(2,1)}, f32[2,128]{1,0:T(2,128)}) custom-call(bf16[4224,128]{1,0:T(8,128)(2,1)S(1)} %bitcast.66), custom_call_target="tpu_custom_call" | custom-call | tf_op jit(solution)/shard_map/pallas_call | solution.py:179
  (6 shorter events, 0.1 us)
Async XLA Ops:
  0.6 28.1 %copy-start = (bf16[2,12,128,128]{3,2,1,0:T(8,128)(2,1)S(1)}, bf16[2,12,128,128]{3,2,1,0:T(8,128)(2,1)}, u32[]{:S(2)}) copy-start(bf16[2,12,128,128]{3,2,1,0:T(8,128)(2,1)} %param.13) | copy-start | bytes 2359300
  3.8 19.8 %copy-start.3 = (bf16[64,2,2,16,128]{4,3,2,1,0:T(8,128)(2,1)S(1)}, bf16[64,2,2,16,128]{4,3,2,1,0:T(8,128)(2,1)}, u32[]{:S(2)}) copy-start(bf16[64,2,2,16,128]{4,3,2,1,0:T(8,128)(2,1)} %get-tuple-element.10) | copy-start | bytes 3145732
  3.8 19.8 %copy-start.6 = (bf16[2,2,128,128]{3,2,1,0:T(8,128)(2,1)S(1)}, bf16[2,2,128,128]{3,2,1,0:T(8,128)(2,1)}, u32[]{:S(2)}) copy-start(bf16[2,2,128,128]{3,2,1,0:T(8,128)(2,1)} %param.23) | copy-start | bytes 393220
  3.8 71.5 %all-to-all-start = ((bf16[64,2,2,16,128]{4,3,2,1,0:T(8,128)(2,1)}), bf16[64,2,2,16,128]{4,3,2,1,0:T(8,128)(2,1)S(1)}, u32[]{:S(2)}, u32[]{:S(2)}) async-start(bf16[64,2,2,16,128]{4,3,2,1,0:T(8,128)(2,1)} %get-tuple-element.10), calls=%async_computation | async-start | bytes 2097152 | tf_op jit(solution)/shard_map/all_to_all | solution.py:215
  23.6 5.0 %copy-start.4 = (bf16[2,4,12,1024]{3,1,2,0:T(4,128)(2,1)S(1)}, bf16[2,4,12,1024]{3,1,2,0:T(4,128)(2,1)}, u32[]{:S(2)}) copy-start(bf16[2,4,12,1024]{3,1,2,0:T(4,128)(2,1)} %param.12) | copy-start | bytes 589828
  24.1 5.3 %copy-start.7 = (bf16[2,4,12,128]{3,1,2,0:T(4,128)(2,1)S(1)}, bf16[2,4,12,128]{3,1,2,0:T(4,128)(2,1)}, u32[]{:S(2)}) copy-start(bf16[2,4,12,128]{3,1,2,0:T(4,128)(2,1)} %param.15) | copy-start | bytes 73732
  24.2 8.0 %collective-permute-start = (f32[128,128]{1,0:T(8,128)S(1)}, f32[128,128]{1,0:T(8,128)S(1)}, u32[]{:S(2)}, u32[]{:S(2)}) collective-permute-start(f32[128,128]{1,0:T(8,128)S(1)} %fusion.18), channel_id=1, source_target_pairs={{0,1},{1,0},{2,3},{3,2},{4,5},{5,4},{6,7},{7,6},{8,9},{9,8},{10,11... | collective-permute-start | bytes 196616 | tf_op jit(solution)/shard_map/ppermute | solution.py:225
  28.7 5.9 %copy-start.5 = (bf16[2,12,128,128]{3,2,1,0:T(8,128)(2,1)S(1)}, bf16[2,12,128,128]{3,2,1,0:T(8,128)(2,1)}, u32[]{:S(2)}) copy-start(bf16[2,12,128,128]{3,2,1,0:T(8,128)(2,1)} %param.14) | copy-start | bytes 2359300
  32.3 8.2 %copy-start.8 = (bf16[2,4,12,128]{3,1,2,0:T(4,128)(2,1)S(1)}, bf16[2,4,12,128]{3,1,2,0:T(4,128)(2,1)}, u32[]{:S(2)}) copy-start(bf16[2,4,12,128]{3,1,2,0:T(4,128)(2,1)} %param.16) | copy-start | bytes 73732
  32.3 5.3 %collective-permute-start.1 = (f32[128,128]{1,0:T(8,128)S(1)}, f32[128,128]{1,0:T(8,128)S(1)}, u32[]{:S(2)}, u32[]{:S(2)}) collective-permute-start(f32[128,128]{1,0:T(8,128)S(1)} %add.27), channel_id=1, source_target_pairs={{0,2},{1,3},{2,0},{3,1},{4,6},{5,7},{6,4},{7,5},{8,10},{9,11},{10,... | collective-permute-start | bytes 196616 | tf_op jit(solution)/shard_map/ppermute | solution.py:225
  35.1 40.2 %copy-start.1 = (s32[64]{0:T(128)S(1)}, s32[64]{0:T(128)}, u32[]{:S(2)}) copy-start(s32[64]{0:T(128)} %source_ref.1) | copy-start | bytes 772
  35.1 40.2 %copy-start.2 = (s32[64]{0:T(128)S(1)}, s32[64]{0:T(128)}, u32[]{:S(2)}) copy-start(s32[64]{0:T(128)} %target_ref.1) | copy-start | bytes 772
  37.6 6.8 %collective-permute-start.2 = (f32[128,128]{1,0:T(8,128)S(1)}, f32[128,128]{1,0:T(8,128)S(1)}, u32[]{:S(2)}, u32[]{:S(2)}) collective-permute-start(f32[128,128]{1,0:T(8,128)S(1)} %add.28), channel_id=1, source_target_pairs={{0,4},{1,5},{2,6},{3,7},{4,0},{5,1},{6,2},{7,3},{8,12},{9,13},{10,... | collective-permute-start | bytes 196616 | tf_op jit(solution)/shard_map/ppermute | solution.py:225

commit v7 on v6

--- a/solution.py
+++ b/solution.py
@@ -54,7 +54,7 @@
 
 
 def take_kernel(
-    source_hbm, length_hbm, list_hbm, pool_hbm, own_ref, out_hbm, source, lengths, lists, pool, stage, sems
+    source_hbm, length_hbm, list_hbm, pool_hbm, own_ref, stage, source, lengths, lists, pool, sems
 ):
     fetches = [
         pltpu.make_async_copy(*pair, sems.at[n])
@@ -66,7 +66,6 @@
         fetch.start()
     place = lax.axis_index("inst")
     depth, span = stage.shape[0], stage.shape[3]
-    rows = depth // 4
     fetches[0].wait()
     own = jnp.int32(0)
     for i in range(source.shape[0]):
@@ -82,16 +81,9 @@
         stage[b] = jnp.where(token < length, block.astype(jnp.float32), 0.0).astype(block.dtype)
         return carry
 
-    writes = []
-    for n in range(depth // rows):
-        for b in range(n * rows, (n + 1) * rows):
-            stage[b] = pool[lists[own, b]]
-        lax.fori_loop(jnp.maximum(length // span, n * rows), (n + 1) * rows, clear, 0)
-        part = pl.ds(n * rows, rows)
-        writes.append(pltpu.make_async_copy(stage.at[part], out_hbm.at[part], sems.at[4 + n]))
-        writes[-1].start()
-    for write in writes:
-        write.wait()
+    for b in range(depth):
+        stage[b] = pool[lists[own, b]]
+    lax.fori_loop(length // span, depth, clear, 0)
 
 
 def take_blocks(mig_source, mig_lengths, block_lists, kv_pool):
@@ -101,7 +93,7 @@
         in_specs=[pl.BlockSpec(memory_space=pltpu.HBM)] * 4,
         out_specs=[
             pl.BlockSpec(memory_space=pltpu.SMEM),
-            pl.BlockSpec(memory_space=pltpu.HBM),
+            pl.BlockSpec(memory_space=pltpu.VMEM),
         ],
         out_shape=[
             jax.ShapeDtypeStruct((1,), jnp.int32),
@@ -112,8 +104,7 @@
             pltpu.SMEM(mig_lengths.shape, jnp.int32),
             pltpu.SMEM(block_lists.shape, jnp.int32),
             pltpu.VMEM(kv_pool.shape, kv_pool.dtype),
-            pltpu.VMEM((depth,) + kv_pool.shape[1:], kv_pool.dtype),
-            pltpu.SemaphoreType.DMA((8,)),
+            pltpu.SemaphoreType.DMA((4,)),
         ],
         compiler_params=pltpu.CompilerParams(vmem_limit_bytes=60 * 1024 * 1024),
     )(mig_source, mig_lengths, block_lists, kv_pool)
@@ -152,11 +143,10 @@
     )(mig_source, mig_target, held, terms)
 
 
-def split_kernel(landed_ref, arrived_hbm, sums_ref, stage, sems):
+def split_kernel(landed_ref, stage, sums_ref):
     depth, rows = stage.shape[:2]
     group = 8
     total = jnp.zeros(sums_ref.shape, jnp.float32)
-    writes = []
     for first in range(0, depth, group):
         size = (rows + SLOTS) * group
         whole = landed_ref[pl.ds(first * (rows + SLOTS), size)]
@@ -164,12 +154,7 @@
             base = j * (rows + SLOTS)
             stage[first + j] = whole[base : base + rows].astype(stage.dtype)
             total = total + whole[base + rows : base + rows + SLOTS].astype(jnp.float32)
-        part = pl.ds(first, group)
-        writes.append(pltpu.make_async_copy(stage.at[part], arrived_hbm.at[part], sems.at[first // group]))
-        writes[-1].start()
     sums_ref[...] = total
-    for write in writes:
-        write.wait()
 
 
 def split_landed(landed, depth):
@@ -179,14 +164,10 @@
     return pl.pallas_call(
         split_kernel,
         in_specs=[vmem],
-        out_specs=[pl.BlockSpec(memory_space=pl.ANY), vmem],
+        out_specs=[vmem, vmem],
         out_shape=[
             jax.ShapeDtypeStruct((depth, rows, width), landed.dtype),
             jax.ShapeDtypeStruct((SLOTS, width), jnp.float32),
-        ],
-        scratch_shapes=[
-            pltpu.VMEM((depth, rows, width), landed.dtype),
-            pltpu.SemaphoreType.DMA((depth // 8,)),
         ],
         compiler_params=pltpu.CompilerParams(vmem_limit_bytes=16 * 1024 * 1024),
     )(landed)

time: 139 us -> 139 us (level)
  no operation moved by 1% of the time
where the time goes in v7:
time: 139 us; the launch traced here: 138 us
  blocking collectives  61.2 us (44%)
  waiting for transfers between devices  37.5 us (27%)
  starting transfers between devices  26.7 us (19%)
  Pallas kernels  4.85 us (3%)
  matrix products  2.98 us (2%)
  between operations  2.79 us (2%)
  local copies, waits for them, and re-layouts  1.56 us (1%)
    all_to_all x1, blocking collectives, local(): lax.all_to_all(onward.reshape(members, -1, SLOTS, width), 'inst', split_a...  61.2 us
    all_to_all x1, waiting for transfers between devices, local(): lax.all_to_all(blocks, 'inst', split_axis=0, concat_axis=0, tiled=True)  30.8 us
    all_to_all x1, starting transfers between devices, local(): lax.all_to_all(blocks, 'inst', split_axis=0, concat_axis=0, tiled=True)  17.1 us
    ppermute x3, starting transfers between devices, local(): lax.ppermute(table, 'tp', [(i, i ^ reach) for i in range(heads)])  9.59 us
    ppermute x3, waiting for transfers between devices, local(): lax.ppermute(table, 'tp', [(i, i ^ reach) for i in range(heads)])  6.63 us
    pallas_call x1, Pallas kernels, take_blocks(): pl.pallas_call(take_kernel, in_specs=[pl.BlockSpec(memory_space=pltpu.HBM...  2.84 us
  transfers between devices with their start and end apart: 4, of which 4 were waited for; matrix products, arithmetic and copies ran while one was open for 4% of the time, Pallas kernels for 0%

profile of v7, /device:TPU:57, one launch (start us, length us, event | category | flops | bytes accessed | tf_op | source)
XLA Modules:
  0.0 138.2 jit_solution(3192965395467037964)
XLA Ops:
  0.6 0.0 copy-start
  0.6 2.8 %shard_map.139 = (s32[1]{0:T(128)}, bf16[64,2,2,16,128]{4,3,2,1,0:T(8,128)(2,1)}) custom-call(s32[64]{0:T(128)} %source_ref.1, s32[64]{0:T(128)} %length_hbm.1, s32[64,64]{1,0:T(8,128)} %list_hbm.1, bf16[80,2,2,16,128]{4,3,2,1,0:T(8,128)(2,1)} %pool_hbm.1), custom_call_target="tpu_custom_call" | custom-call | tf_op jit(solution)/shard_map/pallas_call | solution.py:91
  3.5 0.0 copy-start.3
  3.5 0.0 copy-start.6
  3.5 17.1 %all-to-all-start = ((bf16[64,2,2,16,128]{4,3,2,1,0:T(8,128)(2,1)}), bf16[64,2,2,16,128]{4,3,2,1,0:T(8,128)(2,1)S(1)}, u32[]{:S(2)}, u32[]{:S(2)}) async-start(bf16[64,2,2,16,128]{4,3,2,1,0:T(8,128)(2,1)} %get-tuple-element.10), calls=%async_computation | async-start | bytes 2097152 | tf_op jit(solution)/shard_map/all_to_all | solution.py:196
  22.6 0.7 dynamic-slice_bitcast_fusion
  23.3 0.0 copy-done.3
  23.3 0.0 copy-done.6
  23.3 0.0 copy-start.4
  23.3 0.5 tanh_reduce_fusion
  23.8 0.0 copy-start.7
  23.8 0.2 fusion.18
  24.0 4.4 %collective-permute-start = (f32[128,128]{1,0:T(8,128)S(1)}, f32[128,128]{1,0:T(8,128)S(1)}, u32[]{:S(2)}, u32[]{:S(2)}) collective-permute-start(f32[128,128]{1,0:T(8,128)S(1)} %fusion.18), channel_id=1, source_target_pairs={{0,1},{1,0},{2,3},{3,2},{4,5},{5,4},{6,7},{7,6},{8,9},{9,8},{10,11... | collective-permute-start | bytes 196616 | tf_op jit(solution)/shard_map/ppermute | solution.py:206
  28.3 0.0 copy-done.4
  28.3 0.1 reshape.102
  28.4 0.0 copy-done
  28.5 0.0 copy-start.5
  28.5 0.6 fusion.26
  29.1 0.0 copy-done.7
  29.1 1.0 fusion.27
  30.1 0.4 fusion.9
  30.5 0.2 fusion.13
  30.7 1.3 collective-permute-done
  32.0 0.0 copy-start.8
  32.0 2.4 %collective-permute-start.1 = (f32[128,128]{1,0:T(8,128)S(1)}, f32[128,128]{1,0:T(8,128)S(1)}, u32[]{:S(2)}, u32[]{:S(2)}) collective-permute-start(f32[128,128]{1,0:T(8,128)S(1)} %add.27), channel_id=1, source_target_pairs={{0,2},{1,3},{2,0},{3,1},{4,6},{5,7},{6,4},{7,5},{8,10},{9,11},{10,... | collective-permute-start | bytes 196616 | tf_op jit(solution)/shard_map/ppermute | solution.py:206
  34.4 0.0 copy-done.5
  34.4 0.4 fusion.6
  34.8 0.0 copy-start.1
  34.8 0.0 copy-start.2
  34.8 2.5 %collective-permute-done.1 = f32[128,128]{1,0:T(8,128)S(1)} collective-permute-done((f32[128,128]{1,0:T(8,128)S(1)}, f32[128,128]{1,0:T(8,128)S(1)}, u32[]{:S(2)}, u32[]{:S(2)}) %collective-permute-start.1) | collective-permute-done | bytes 65568 | tf_op jit(solution)/shard_map/ppermute | solution.py:206
  37.3 2.9 %collective-permute-start.2 = (f32[128,128]{1,0:T(8,128)S(1)}, f32[128,128]{1,0:T(8,128)S(1)}, u32[]{:S(2)}, u32[]{:S(2)}) collective-permute-start(f32[128,128]{1,0:T(8,128)S(1)} %add.28), channel_id=1, source_target_pairs={{0,4},{1,5},{2,6},{3,7},{4,0},{5,1},{6,2},{7,3},{8,12},{9,13},{10,... | collective-permute-start | bytes 196616 | tf_op jit(solution)/shard_map/ppermute | solution.py:206
  40.2 0.0 copy-done.8
  40.2 0.3 fusion.2
  40.6 0.7 reshape.105
  41.3 2.9 %collective-permute-done.2 = f32[128,128]{1,0:T(8,128)S(1)} collective-permute-done((f32[128,128]{1,0:T(8,128)S(1)}, f32[128,128]{1,0:T(8,128)S(1)}, u32[]{:S(2)}, u32[]{:S(2)}) %collective-permute-start.2) | collective-permute-done | bytes 65568 | tf_op jit(solution)/shard_map/ppermute | solution.py:206
  44.2 30.8 %all-to-all-done = bf16[64,2,2,16,128]{4,3,2,1,0:T(8,128)(2,1)S(1)} async-done(((bf16[64,2,2,16,128]{4,3,2,1,0:T(8,128)(2,1)}), bf16[64,2,2,16,128]{4,3,2,1,0:T(8,128)(2,1)S(1)}, u32[]{:S(2)}, u32[]{:S(2)}) %all-to-all-start) | async-done | bytes 1048608 | tf_op jit(solution)/shard_map/all_to_all | solution.py:196
  75.0 0.0 copy-done.1
  75.0 0.0 copy-done.2
  75.0 0.8 shard_map.140
  75.8 61.2 %all_to_all.10 = bf16[64,33,2,128]{3,2,1,0:T(2,128)(2,1)S(1)} all-to-all(bf16[64,33,2,128]{3,2,1,0:T(2,128)(2,1)S(1)} %bitcast.67), channel_id=1, replica_groups=mesh['inst'=64,'tp'=8] {'inst'}, dimensions={0} | all-to-all | bytes 2162688 | tf_op jit(solution)/shard_map/all_to_all | solution.py:213
  137.0 1.2 shard_map.141
  (6 shorter events, 0.1 us)
Async XLA Ops:
  0.6 27.8 %copy-start = (bf16[2,12,128,128]{3,2,1,0:T(8,128)(2,1)S(1)}, bf16[2,12,128,128]{3,2,1,0:T(8,128)(2,1)}, u32[]{:S(2)}) copy-start(bf16[2,12,128,128]{3,2,1,0:T(8,128)(2,1)} %param.13) | copy-start | bytes 2359300
  3.5 19.8 %copy-start.3 = (bf16[64,2,2,16,128]{4,3,2,1,0:T(8,128)(2,1)S(1)}, bf16[64,2,2,16,128]{4,3,2,1,0:T(8,128)(2,1)}, u32[]{:S(2)}) copy-start(bf16[64,2,2,16,128]{4,3,2,1,0:T(8,128)(2,1)} %get-tuple-element.10) | copy-start | bytes 3145732
  3.5 19.8 %copy-start.6 = (bf16[2,2,128,128]{3,2,1,0:T(8,128)(2,1)S(1)}, bf16[2,2,128,128]{3,2,1,0:T(8,128)(2,1)}, u32[]{:S(2)}) copy-start(bf16[2,2,128,128]{3,2,1,0:T(8,128)(2,1)} %param.23) | copy-start | bytes 393220
  3.5 71.5 %all-to-all-start = ((bf16[64,2,2,16,128]{4,3,2,1,0:T(8,128)(2,1)}), bf16[64,2,2,16,128]{4,3,2,1,0:T(8,128)(2,1)S(1)}, u32[]{:S(2)}, u32[]{:S(2)}) async-start(bf16[64,2,2,16,128]{4,3,2,1,0:T(8,128)(2,1)} %get-tuple-element.10), calls=%async_computation | async-start | bytes 2097152 | tf_op jit(solution)/shard_map/all_to_all | solution.py:196
  23.3 5.0 %copy-start.4 = (bf16[2,4,12,1024]{3,1,2,0:T(4,128)(2,1)S(1)}, bf16[2,4,12,1024]{3,1,2,0:T(4,128)(2,1)}, u32[]{:S(2)}) copy-start(bf16[2,4,12,1024]{3,1,2,0:T(4,128)(2,1)} %param.12) | copy-start | bytes 589828
  23.8 5.3 %copy-start.7 = (bf16[2,4,12,128]{3,1,2,0:T(4,128)(2,1)S(1)}, bf16[2,4,12,128]{3,1,2,0:T(4,128)(2,1)}, u32[]{:S(2)}) copy-start(bf16[2,4,12,128]{3,1,2,0:T(4,128)(2,1)} %param.15) | copy-start | bytes 73732
  24.0 8.0 %collective-permute-start = (f32[128,128]{1,0:T(8,128)S(1)}, f32[128,128]{1,0:T(8,128)S(1)}, u32[]{:S(2)}, u32[]{:S(2)}) collective-permute-start(f32[128,128]{1,0:T(8,128)S(1)} %fusion.18), channel_id=1, source_target_pairs={{0,1},{1,0},{2,3},{3,2},{4,5},{5,4},{6,7},{7,6},{8,9},{9,8},{10,11... | collective-permute-start | bytes 196616 | tf_op jit(solution)/shard_map/ppermute | solution.py:206
  28.5 6.0 %copy-start.5 = (bf16[2,12,128,128]{3,2,1,0:T(8,128)(2,1)S(1)}, bf16[2,12,128,128]{3,2,1,0:T(8,128)(2,1)}, u32[]{:S(2)}) copy-start(bf16[2,12,128,128]{3,2,1,0:T(8,128)(2,1)} %param.14) | copy-start | bytes 2359300
  32.0 8.2 %copy-start.8 = (bf16[2,4,12,128]{3,1,2,0:T(4,128)(2,1)S(1)}, bf16[2,4,12,128]{3,1,2,0:T(4,128)(2,1)}, u32[]{:S(2)}) copy-start(bf16[2,4,12,128]{3,1,2,0:T(4,128)(2,1)} %param.16) | copy-start | bytes 73732
  32.0 5.3 %collective-permute-start.1 = (f32[128,128]{1,0:T(8,128)S(1)}, f32[128,128]{1,0:T(8,128)S(1)}, u32[]{:S(2)}, u32[]{:S(2)}) collective-permute-start(f32[128,128]{1,0:T(8,128)S(1)} %add.27), channel_id=1, source_target_pairs={{0,2},{1,3},{2,0},{3,1},{4,6},{5,7},{6,4},{7,5},{8,10},{9,11},{10,... | collective-permute-start | bytes 196616 | tf_op jit(solution)/shard_map/ppermute | solution.py:206
  34.8 40.2 %copy-start.1 = (s32[64]{0:T(128)S(1)}, s32[64]{0:T(128)}, u32[]{:S(2)}) copy-start(s32[64]{0:T(128)} %source_ref.1) | copy-start | bytes 772
  34.8 40.2 %copy-start.2 = (s32[64]{0:T(128)S(1)}, s32[64]{0:T(128)}, u32[]{:S(2)}) copy-start(s32[64]{0:T(128)} %target_ref.1) | copy-start | bytes 772
  37.3 6.8 %collective-permute-start.2 = (f32[128,128]{1,0:T(8,128)S(1)}, f32[128,128]{1,0:T(8,128)S(1)}, u32[]{:S(2)}, u32[]{:S(2)}) collective-permute-start(f32[128,128]{1,0:T(8,128)S(1)} %add.28), channel_id=1, source_target_pairs={{0,4},{1,5},{2,6},{3,7},{4,0},{5,1},{6,2},{7,3},{8,12},{9,13},{10,... | collective-permute-start | bytes 196616 | tf_op jit(solution)/shard_map/ppermute | solution.py:206

commit v8 on v7

--- a/solution.py
+++ b/solution.py
@@ -110,14 +110,12 @@
     )(mig_source, mig_lengths, block_lists, kv_pool)
 
 
-def relay_kernel(source_ref, target_ref, held_ref, terms_ref, out_ref, source_of):
+def relay_kernel(source_of, held_ref, terms_ref, out_ref):
     depth = held_ref.shape[0]
     rows = held_ref.shape[1]
     group = 8
 
     terms = terms_ref[...]
-    for r in range(depth):
-        source_of[target_ref[r]] = source_ref[r]
     for first in range(0, depth, group):
         pieces = []
         for t in range(first, first + group):
@@ -128,19 +126,18 @@
         out_ref[pl.ds(first * (rows + SLOTS), size)] = whole.astype(out_ref.dtype)
 
 
-def order_by_target(mig_source, mig_target, held, terms):
+def order_by_target(source_of, held, terms):
     smem = pl.BlockSpec(memory_space=pltpu.SMEM)
     vmem = pl.BlockSpec(memory_space=pltpu.VMEM)
     return pl.pallas_call(
         relay_kernel,
-        in_specs=[smem, smem, vmem, vmem],
+        in_specs=[smem, vmem, vmem],
         out_specs=vmem,
         out_shape=jax.ShapeDtypeStruct(
             (held.shape[0] * (held.shape[1] + SLOTS), held.shape[2]), held.dtype
         ),
-        scratch_shapes=[pltpu.SMEM(mig_target.shape, jnp.int32)],
         compiler_params=pltpu.CompilerParams(vmem_limit_bytes=16 * 1024 * 1024),
-    )(mig_source, mig_target, held, terms)
+    )(source_of, held, terms)
 
 
 def split_kernel(landed_ref, stage, sums_ref):
@@ -207,9 +204,12 @@
         reach *= 2
     terms = table.astype(jnp.bfloat16)
 
-    terms, attention = lax.optimization_barrier((terms, attention))
-
-    onward = order_by_target(mig_source, mig_target, sectioned.reshape(members, -1, width), terms)
+    source_of = jnp.sum(
+        jnp.where(mig_target[None, :] == jnp.arange(members)[:, None], mig_source[None, :], 0), axis=1
+    )
+    terms, attention, source_of = lax.optimization_barrier((terms, attention, source_of))
+
+    onward = order_by_target(source_of, sectioned.reshape(members, -1, width), terms)
     landed = lax.all_to_all(
         onward.reshape(members, -1, SLOTS, width), "inst", split_axis=0, concat_axis=0, tiled=True
     )

time: 139 us -> 139 us (level)
  no operation moved by 1% of the time
where the time goes in v8:
time: 139 us; the launch traced here: 138 us
  blocking collectives  61.2 us (44%)
  waiting for transfers between devices  37.3 us (27%)
  starting transfers between devices  27.1 us (19%)
  Pallas kernels  4.43 us (3%)
  matrix products  2.98 us (2%)
  between operations  2.8 us (2%)
  local copies, waits for them, and re-layouts  1.56 us (1%)
    all_to_all x1, blocking collectives, local(): lax.all_to_all(onward.reshape(members, -1, SLOTS, width), 'inst', split_a...  61.2 us
    all_to_all x1, waiting for transfers between devices, local(): lax.all_to_all(blocks, 'inst', split_axis=0, concat_axis=0, tiled=True)  30.9 us
    all_to_all x1, starting transfers between devices, local(): lax.all_to_all(blocks, 'inst', split_axis=0, concat_axis=0, tiled=True)  17.5 us
    ppermute x3, starting transfers between devices, local(): lax.ppermute(table, 'tp', [(i, i ^ reach) for i in range(heads)])  9.59 us
    ppermute x3, waiting for transfers between devices, local(): lax.ppermute(table, 'tp', [(i, i ^ reach) for i in range(heads)])  6.49 us
  transfers between devices with their start and end apart: 4, of which 4 were waited for; matrix products, arithmetic and copies ran while one was open for 4% of the time, Pallas kernels for 0%

profile of v8, /device:TPU:57, one launch (start us, length us, event | category | flops | bytes accessed | tf_op | source)
XLA Modules:
  0.0 138.1 jit_solution(8996910639616187658)
XLA Ops:
  0.6 0.0 copy-start
  0.6 2.5 %shard_map.139 = (s32[1]{0:T(128)}, bf16[64,2,2,16,128]{4,3,2,1,0:T(8,128)(2,1)}) custom-call(s32[64]{0:T(128)} %source_hbm.1, s32[64]{0:T(128)} %length_hbm.1, s32[64,64]{1,0:T(8,128)} %list_hbm.1, bf16[80,2,2,16,128]{4,3,2,1,0:T(8,128)(2,1)} %pool_hbm.1), custom_call_target="tpu_custom_call" | custom-call | tf_op jit(solution)/shard_map/pallas_call | solution.py:91
  3.2 0.0 copy-start.1
  3.2 0.0 copy-start.5
  3.2 17.5 %all-to-all-start = ((bf16[64,2,2,16,128]{4,3,2,1,0:T(8,128)(2,1)}), bf16[64,2,2,16,128]{4,3,2,1,0:T(8,128)(2,1)S(1)}, u32[]{:S(2)}, u32[]{:S(2)}) async-start(bf16[64,2,2,16,128]{4,3,2,1,0:T(8,128)(2,1)} %get-tuple-element.11), calls=%async_computation | async-start | bytes 2097152 | tf_op jit(solution)/shard_map/all_to_all | solution.py:193
  22.6 0.7 dynamic-slice_bitcast_fusion
  23.3 0.0 copy-done.1
  23.3 0.0 copy-done.5
  23.3 0.0 copy-start.2
  23.3 0.5 tanh_reduce_fusion
  23.8 0.0 copy-start.6
  23.8 0.2 fusion.18
  24.0 4.4 %collective-permute-start = (f32[128,128]{1,0:T(8,128)S(1)}, f32[128,128]{1,0:T(8,128)S(1)}, u32[]{:S(2)}, u32[]{:S(2)}) collective-permute-start(f32[128,128]{1,0:T(8,128)S(1)} %fusion.18), channel_id=1, source_target_pairs={{0,1},{1,0},{2,3},{3,2},{4,5},{5,4},{6,7},{7,6},{8,9},{9,8},{10,11... | collective-permute-start | bytes 196616 | tf_op jit(solution)/shard_map/ppermute | solution.py:203
  28.3 0.0 copy-done.2
  28.3 0.1 reshape.104
  28.4 0.0 copy-done
  28.5 0.0 copy-start.4
  28.5 0.6 fusion.26
  29.1 0.0 copy-done.6
  29.1 1.0 fusion.27
  30.1 0.2 fusion.13
  30.3 0.4 fusion.9
  30.7 0.0 copy-done.4
  30.7 0.0 copy-start.7
  30.7 0.4 fusion.6
  31.1 0.0 copy-start.3
  31.2 0.0 copy-start.8
  31.2 0.8 collective-permute-done
  32.0 2.4 %collective-permute-start.1 = (f32[128,128]{1,0:T(8,128)S(1)}, f32[128,128]{1,0:T(8,128)S(1)}, u32[]{:S(2)}, u32[]{:S(2)}) collective-permute-start(f32[128,128]{1,0:T(8,128)S(1)} %add.27), channel_id=1, source_target_pairs={{0,2},{1,3},{2,0},{3,1},{4,6},{5,7},{6,4},{7,5},{8,10},{9,11},{10,... | collective-permute-start | bytes 196616 | tf_op jit(solution)/shard_map/ppermute | solution.py:203
  34.4 0.0 copy-done.7
  34.4 0.3 fusion.2
  34.7 0.7 reshape.107
  35.5 1.8 %collective-permute-done.1 = f32[128,128]{1,0:T(8,128)S(1)} collective-permute-done((f32[128,128]{1,0:T(8,128)S(1)}, f32[128,128]{1,0:T(8,128)S(1)}, u32[]{:S(2)}, u32[]{:S(2)}) %collective-permute-start.1) | collective-permute-done | bytes 65568 | tf_op jit(solution)/shard_map/ppermute | solution.py:203
  37.3 2.9 %collective-permute-start.2 = (f32[128,128]{1,0:T(8,128)S(1)}, f32[128,128]{1,0:T(8,128)S(1)}, u32[]{:S(2)}, u32[]{:S(2)}) collective-permute-start(f32[128,128]{1,0:T(8,128)S(1)} %add.28), channel_id=1, source_target_pairs={{0,4},{1,5},{2,6},{3,7},{4,0},{5,1},{6,2},{7,3},{8,12},{9,13},{10,... | collective-permute-start | bytes 196616 | tf_op jit(solution)/shard_map/ppermute | solution.py:203
  40.2 0.0 copy-done.3
  40.2 0.0 copy-done.8
  40.2 0.1 select_reduce_fusion.source_of
  40.3 3.8 %collective-permute-done.2 = f32[128,128]{1,0:T(8,128)S(1)} collective-permute-done((f32[128,128]{1,0:T(8,128)S(1)}, f32[128,128]{1,0:T(8,128)S(1)}, u32[]{:S(2)}, u32[]{:S(2)}) %collective-permute-start.2) | collective-permute-done | bytes 65568 | tf_op jit(solution)/shard_map/ppermute | solution.py:203
  44.2 30.9 %all-to-all-done = bf16[64,2,2,16,128]{4,3,2,1,0:T(8,128)(2,1)S(1)} async-done(((bf16[64,2,2,16,128]{4,3,2,1,0:T(8,128)(2,1)}), bf16[64,2,2,16,128]{4,3,2,1,0:T(8,128)(2,1)S(1)}, u32[]{:S(2)}, u32[]{:S(2)}) %all-to-all-start) | async-done | bytes 1048608 | tf_op jit(solution)/shard_map/all_to_all | solution.py:193
  75.0 0.7 shard_map.140
  75.7 61.2 %all_to_all.10 = bf16[64,33,2,128]{3,2,1,0:T(2,128)(2,1)S(1)} all-to-all(bf16[64,33,2,128]{3,2,1,0:T(2,128)(2,1)S(1)} %bitcast.66), channel_id=1, replica_groups=mesh['inst'=64,'tp'=8] {'inst'}, dimensions={0} | all-to-all | bytes 2162688 | tf_op jit(solution)/shard_map/all_to_all | solution.py:213
  136.9 1.2 shard_map.141
  (6 shorter events, 0.1 us)
Async XLA Ops:
  0.6 27.8 %copy-start = (bf16[2,12,128,128]{3,2,1,0:T(8,128)(2,1)S(1)}, bf16[2,12,128,128]{3,2,1,0:T(8,128)(2,1)}, u32[]{:S(2)}) copy-start(bf16[2,12,128,128]{3,2,1,0:T(8,128)(2,1)} %param.13) | copy-start | bytes 2359300
  3.2 20.1 %copy-start.1 = (bf16[64,2,2,16,128]{4,3,2,1,0:T(8,128)(2,1)S(1)}, bf16[64,2,2,16,128]{4,3,2,1,0:T(8,128)(2,1)}, u32[]{:S(2)}) copy-start(bf16[64,2,2,16,128]{4,3,2,1,0:T(8,128)(2,1)} %get-tuple-element.11) | copy-start | bytes 3145732
  3.2 20.1 %copy-start.5 = (bf16[2,2,128,128]{3,2,1,0:T(8,128)(2,1)S(1)}, bf16[2,2,128,128]{3,2,1,0:T(8,128)(2,1)}, u32[]{:S(2)}) copy-start(bf16[2,2,128,128]{3,2,1,0:T(8,128)(2,1)} %param.23) | copy-start | bytes 393220
  3.2 71.8 %all-to-all-start = ((bf16[64,2,2,16,128]{4,3,2,1,0:T(8,128)(2,1)}), bf16[64,2,2,16,128]{4,3,2,1,0:T(8,128)(2,1)S(1)}, u32[]{:S(2)}, u32[]{:S(2)}) async-start(bf16[64,2,2,16,128]{4,3,2,1,0:T(8,128)(2,1)} %get-tuple-element.11), calls=%async_computation | async-start | bytes 2097152 | tf_op jit(solution)/shard_map/all_to_all | solution.py:193
  23.3 5.0 %copy-start.2 = (bf16[2,4,12,1024]{3,1,2,0:T(4,128)(2,1)S(1)}, bf16[2,4,12,1024]{3,1,2,0:T(4,128)(2,1)}, u32[]{:S(2)}) copy-start(bf16[2,4,12,1024]{3,1,2,0:T(4,128)(2,1)} %param.12) | copy-start | bytes 589828
  23.8 5.3 %copy-start.6 = (bf16[2,4,12,128]{3,1,2,0:T(4,128)(2,1)S(1)}, bf16[2,4,12,128]{3,1,2,0:T(4,128)(2,1)}, u32[]{:S(2)}) copy-start(bf16[2,4,12,128]{3,1,2,0:T(4,128)(2,1)} %param.15) | copy-start | bytes 73732
  24.0 8.0 %collective-permute-start = (f32[128,128]{1,0:T(8,128)S(1)}, f32[128,128]{1,0:T(8,128)S(1)}, u32[]{:S(2)}, u32[]{:S(2)}) collective-permute-start(f32[128,128]{1,0:T(8,128)S(1)} %fusion.18), channel_id=1, source_target_pairs={{0,1},{1,0},{2,3},{3,2},{4,5},{5,4},{6,7},{7,6},{8,9},{9,8},{10,11... | collective-permute-start | bytes 196616 | tf_op jit(solution)/shard_map/ppermute | solution.py:203
  28.5 2.3 %copy-start.4 = (bf16[2,12,128,128]{3,2,1,0:T(8,128)(2,1)S(1)}, bf16[2,12,128,128]{3,2,1,0:T(8,128)(2,1)}, u32[]{:S(2)}) copy-start(bf16[2,12,128,128]{3,2,1,0:T(8,128)(2,1)} %param.14) | copy-start | bytes 2359300
  30.7 3.7 %copy-start.7 = (bf16[2,4,12,128]{3,1,2,0:T(4,128)(2,1)S(1)}, bf16[2,4,12,128]{3,1,2,0:T(4,128)(2,1)}, u32[]{:S(2)}) copy-start(bf16[2,4,12,128]{3,1,2,0:T(4,128)(2,1)} %param.16) | copy-start | bytes 73732
  31.1 9.1 %copy-start.3 = (s32[64]{0:T(128)S(1)}, s32[64]{0:T(128)}, u32[]{:S(2)}) copy-start(s32[64]{0:T(128)} %source_hbm.1) | copy-start | bytes 772
  31.2 9.1 %copy-start.8 = (s32[64]{0:T(128)S(1)}, s32[64]{0:T(128)}, u32[]{:S(2)}) copy-start(s32[64]{0:T(128)} %param.20) | copy-start | bytes 772
  32.0 5.3 %collective-permute-start.1 = (f32[128,128]{1,0:T(8,128)S(1)}, f32[128,128]{1,0:T(8,128)S(1)}, u32[]{:S(2)}, u32[]{:S(2)}) collective-permute-start(f32[128,128]{1,0:T(8,128)S(1)} %add.27), channel_id=1, source_target_pairs={{0,2},{1,3},{2,0},{3,1},{4,6},{5,7},{6,4},{7,5},{8,10},{9,11},{10,... | collective-permute-start | bytes 196616 | tf_op jit(solution)/shard_map/ppermute | solution.py:203
  37.3 6.8 %collective-permute-start.2 = (f32[128,128]{1,0:T(8,128)S(1)}, f32[128,128]{1,0:T(8,128)S(1)}, u32[]{:S(2)}, u32[]{:S(2)}) collective-permute-start(f32[128,128]{1,0:T(8,128)S(1)} %add.28), channel_id=1, source_target_pairs={{0,4},{1,5},{2,6},{3,7},{4,0},{5,1},{6,2},{7,3},{8,12},{9,13},{10,... | collective-permute-start | bytes 196616 | tf_op jit(solution)/shard_map/ppermute | solution.py:203
